TPU v7x, 256 devices: a whole 4x4x8 slice. The times are simulated.
256 devices in a mesh: row: 8 (over x, z_lo), col: 32 (over z_hi, y, core).
Axes of the slice: x: 4, y: 4, z: 8 (z_hi: 4, z_lo: 2; z = z_hi * 2 + z_lo), core: 2. Of those that a mesh axis runs over, the one named last changes fastest.
Arguments:
- activations: bfloat16 [4096, 2560], P('col', 'row'), may hold values from -6 to 6
- cotangent: bfloat16 [4096, 6912], P('row', 'col'), may hold values from -6 to 6
- small_weight: bfloat16 [2048, 5504], P('row', 'col'), may hold values from -0.125 to 0.125
- grow_rows: bfloat16 [2560, 2048], P('row', 'col'), may hold values from -0.125 to 0.125
- grow_cols: bfloat16 [6912, 5504], P('col', 'row'), may hold values from -0.15625 to 0.15625
Outputs:
- grad_rows: bfloat16 [2560, 2048], P('row', 'col')
- grad_cols: bfloat16 [6912, 5504], P('col', 'row')
- grad_small: bfloat16 [2048, 5504], P('row', 'col')
All inputs are finite; a program needn't handle non-finite values.
Results may differ from a plain program's by a relative error of at most 0.015.
Values may be sent and summed in bfloat16 or wider, within the bound.
A program may use at most 64 MiB of HBM per device.

v0:
```python
import jax
import jax.numpy as jnp
from jax import lax
from jax.sharding import PartitionSpec as P


def contract(left, right, left_dim, right_dim):
    return lax.dot_general(
        left, right, (((left_dim,), (right_dim,)), ((), ())), preferred_element_type=jnp.float32
    )


def local(activations, cotangent, small_weight, grow_rows, grow_cols):
    b_panel = lax.all_gather(grow_cols, "row", axis=1, tiled=True)
    w_panel = lax.all_gather(small_weight, "col", axis=1, tiled=True)
    product = contract(w_panel, b_panel, 1, 1).astype(jnp.bfloat16)
    c_panel = lax.all_gather(product, "row", axis=0, tiled=True)
    a_panel = lax.all_gather(grow_rows, "col", axis=1, tiled=True)
    grown_panel = jnp.dot(a_panel, c_panel, preferred_element_type=jnp.float32).astype(jnp.bfloat16)
    tokens_all = lax.all_gather(activations, "col", axis=0, tiled=True)
    block = tokens_all
    hidden = lax.psum_scatter(
        jnp.dot(block, grown_panel, preferred_element_type=jnp.float32),
        "row",
        scatter_dimension=0,
        tiled=True,
    )
    squash = jax.nn.sigmoid(hidden)
    delta_local = (cotangent.astype(jnp.float32) * squash * (1.0 + hidden * (1.0 - squash))).astype(
        jnp.bfloat16
    )
    delta_all = lax.all_gather(delta_local, "row", axis=0, tiled=True)
    norm_scale = jnp.float32(delta_all.shape[0]) ** (-0.5)
    grad_grown = (contract(tokens_all, delta_all, 0, 0) * norm_scale).astype(jnp.bfloat16)
    block = c_panel
    grad_rows = lax.psum_scatter(
        contract(block, grad_grown, 1, 1), "col", scatter_dimension=0, tiled=True
    ).T.astype(jnp.bfloat16)
    block = a_panel
    back_panel = lax.psum_scatter(
        contract(block, grad_grown, 0, 0), "row", scatter_dimension=0, tiled=True
    ).astype(jnp.bfloat16)
    block = w_panel
    grad_cols = lax.psum_scatter(
        contract(block, back_panel, 0, 0), "row", scatter_dimension=0, tiled=True
    ).T.astype(jnp.bfloat16)
    block = b_panel
    grad_small = lax.psum_scatter(
        contract(block, back_panel, 0, 1), "col", scatter_dimension=0, tiled=True
    ).T.astype(jnp.bfloat16)
    return (grad_rows, grad_cols, grad_small)


def solution(mesh):
    return jax.shard_map(
        local,
        mesh=mesh,
        in_specs=(
            P("col", "row"),
            P("row", "col"),
            P("row", "col"),
            P("row", "col"),
            P("col", "row"),
        ),
        out_specs=(P("row", "col"), P("col", "row"), P("row", "col")),
        check_vma=False,
    )
```

profile of v0, /device:TPU:33, one launch (start us, length us, event | category | flops | bytes accessed | tf_op | source)
XLA Modules:
  0.0 729.3 jit_solution(9134839111984349272)
XLA Ops:
  10.0 65.7 %all-gather.16.cloned.1.call-done = bf16[8,688,216]{1,2,0:T(8,128)(2,1)} async-done(((bf16[1,688,216]{1,2,0:T(8,128)(2,1)}), bf16[8,688,216]{1,2,0:T(8,128)(2,1)}) %all-gather.16.cloned.1.call-update) | async-done | bytes 2377744 | tf_op jit(solution)/shard_map/all_gather | solution.py:14
  75.7 2.3 copy.11
  78.0 3.6 reshape.9
  81.6 53.3 %all-gather.14.cloned.1.call-done = bf16[32,172,256]{2,1,0:T(8,128)(2,1)} async-done(((bf16[1,172,256]{2,1,0:T(8,128)(2,1)}), bf16[32,172,256]{2,1,0:T(8,128)(2,1)}) %all-gather.14.cloned.1.call-update) | async-done | bytes 2818064 | tf_op jit(solution)/shard_map/all_gather | solution.py:15
  134.8 3.6 reshape.7
  138.4 2.5 convolution_convert_fusion.1
  140.9 28.9 %all_gather.20 = bf16[2048,216]{0,1:T(8,128)(2,1)} all-gather(bf16[256,216]{0,1:T(8,128)(2,1)S(1)} %convolution_convert_fusion.1), channel_id=1, replica_groups=mesh['row'=8,'col'=32] {'row'}, dimensions={0}, use_global_device_ids=true | all-gather | bytes 995328 | tf_op jit(solution)/shard_map/all_gather | solution.py:17
  169.8 18.5 %all-gather.8.cloned.1.call-done = bf16[320,2048]{0,1:T(8,128)(2,1)} async-done(((bf16[320,64]{0,1:T(8,128)(2,1)}), bf16[320,2048]{0,1:T(8,128)(2,1)}) %all-gather.8.cloned.1.call-update) | async-done | bytes 1310736 | tf_op jit(solution)/shard_map/all_gather | solution.py:18
  188.3 57.2 %all-gather.10.cloned.1.call-done = bf16[4096,320]{0,1:T(8,128)(2,1)} async-done(((bf16[128,320]{0,1:T(8,128)(2,1)}), bf16[4096,320]{0,1:T(8,128)(2,1)}) %all-gather.10.cloned.1.call-update) | async-done | bytes 2621456 | tf_op jit(solution)/shard_map/all_gather | solution.py:20
  245.5 6.5 convolution_bitcast_fusion.2
  252.1 79.9 %reduce-scatter.8.cloned.1.call-done = f32[512,216]{0,1:T(8,128)} async-done(((f32[4096,216]{0,1:T(8,128)}), f32[512,216]{0,1:T(8,128)}) %reduce-scatter.8.cloned.1.call-update) | async-done | bytes 442384 | tf_op jit(solution)/shard_map/reduce_scatter | solution.py:22
  331.9 1.9 multiply_convert_fusion
  333.9 48.2 %all-gather.12.cloned.1.call-done = bf16[4096,216]{0,1:T(8,128)(2,1)} async-done(((bf16[512,216]{0,1:T(8,128)(2,1)}), bf16[4096,216]{0,1:T(8,128)(2,1)}) %all-gather.12.cloned.1.call-update) | async-done | bytes 1769488 | tf_op jit(solution)/shard_map/all_gather | solution.py:32
  382.1 3.3 fusion
  385.4 2.1 convolution_bitcast_fusion.3
  387.5 3.7 fusion.4
  391.3 44.5 %reduce-scatter.12.cloned.1.call-done = f32[256,216]{0,1:T(8,128)} async-done(((f32[2048,216]{0,1:T(8,128)}), f32[256,216]{0,1:T(8,128)}) %reduce-scatter.12.cloned.1.call-update) | async-done | bytes 221200 | tf_op jit(solution)/shard_map/reduce_scatter | solution.py:40
  435.8 4.2 convolution_bitcast_fusion.1
  440.0 6.0 copy.13
  447.9 3.5 convolution_bitcast_fusion
  451.3 221.6 %all-reduce.2 = bf16[5504,256]{0,1:T(8,128)(2,1)S(1)} all-reduce(f32[5504,256]{0,1:T(8,128)} %convolution_bitcast_fusion), channel_id=6, replica_groups=mesh['row'=8,'col'=32] {'col'}, use_global_device_ids=true, to_apply=%region_4.0.clone | all-reduce | flops 1409024 | bytes 8454144
  673.8 1.5 convert_bitcast_fusion.1
  675.3 45.5 %reduce-scatter.14.cloned.1.call-done = f32[688,216]{1,0:T(8,128)} async-done(((f32[5504,216]{1,0:T(8,128)}), f32[688,216]{1,0:T(8,128)}) %reduce-scatter.14.cloned.1.call-update) | async-done | bytes 594448
  720.8 2.0 copy.14
  (32 shorter events, 5.1 us)
Async XLA Ops:
  7.2 68.6 %all-gather.16.cloned.1.call-start = ((), (), s32[]{:S(2)}) async-start(), calls=%async_computation.11 | async-start | bytes 2985984 | tf_op jit(solution)/shard_map/all_gather | solution.py:14
  7.9 126.9 %all-gather.14.cloned.1.call-start = ((), (), s32[]{:S(2)}) async-start(), calls=%async_computation.10 | async-start | bytes 2973696 | tf_op jit(solution)/shard_map/all_gather | solution.py:15
  8.6 179.6 %all-gather.8.cloned.1.call-start = ((), (), s32[]{:S(2)}) async-start(), calls=%async_computation.4 | async-start | bytes 1622016 | tf_op jit(solution)/shard_map/all_gather | solution.py:18
  9.4 236.1 %all-gather.10.cloned.1.call-start = ((), (), s32[]{:S(2)}) async-start(), calls=%async_computation.5 | async-start | bytes 2703360 | tf_op jit(solution)/shard_map/all_gather | solution.py:20
  10.0 322.0 %reduce-scatter.8.cloned.1.call-start = ((), (), s32[]{:S(2)}) async-start(), calls=%async_computation.6 | async-start | bytes 3981312 | tf_op jit(solution)/shard_map/reduce_scatter | solution.py:22
  252.0 79.9 %copy-start.3 = (bf16[512,216]{0,1:T(8,128)(2,1)S(1)}, bf16[512,216]{0,1:T(8,128)(2,1)}, u32[]{:S(2)}) copy-start(bf16[512,216]{0,1:T(8,128)(2,1)} %param.6) | copy-start | bytes 663556
  252.0 130.1 %all-gather.12.cloned.1.call-start = ((), (), s32[]{:S(2)}) async-start(), calls=%async_computation.7 | async-start | bytes 1990656 | tf_op jit(solution)/shard_map/all_gather | solution.py:32
  333.8 102.0 %reduce-scatter.12.cloned.1.call-start = ((), (), s32[]{:S(2)}) async-start(), calls=%async_computation.9 | async-start | bytes 1990656 | tf_op jit(solution)/shard_map/reduce_scatter | solution.py:40
  382.1 3.3 copy-start.1
  387.5 286.3 %reduce-scatter.10.cloned.1.call-start = ((), (), s32[]{:S(2)}) async-start(), calls=%async_computation.8 | async-start | bytes 3244032 | tf_op jit(solution)/shard_map/reduce_scatter | solution.py:36
  391.2 329.5 %reduce-scatter.14.cloned.1.call-start = ((), (), s32[]{:S(2)}) async-start(), calls=%async_computation.12 | async-start | bytes 6340608
  445.9 0.7 copy-start.4
  445.9 1.9 copy-start
  445.9 1.9 copy-start.2
Sparse Core Ops, SparseCore 0:
  9.8 65.8 all-gather.15
  78.3 56.5 all-gather.13
  137.4 50.8 all-gather.7
  190.6 54.7 all-gather.9
  252.1 79.7 reduce-scatter.7
  334.3 47.7 all-gather.11
  387.6 48.1 reduce-scatter.11
  440.2 102.4 reduce-scatter.9
  545.3 175.4 reduce-scatter.13
where the time goes:
time: 734 us; the launch traced here: 729 us
  waiting for transfers between devices  415 us (57%)
  blocking collectives  250 us (34%)
  matrix products  25.7 us (4%)
  local copies, waits for them, and re-layouts  19.5 us (3%)
  between operations  14.6 us (2%)
    unnamed x1, blocking collectives  222 us
    reduce_scatter x1, waiting for transfers between devices, local(): lax.psum_scatter(jnp.dot(block, grown_panel, preferred_element_type=jnp.f...  79.9 us
    all_gather x1, waiting for transfers between devices, local(): b_panel = lax.all_gather(grow_cols, 'row', axis=1, tiled=True)  65.7 us
    all_gather x1, waiting for transfers between devices, local(): tokens_all = lax.all_gather(activations, 'col', axis=0, tiled=True)  57.2 us
    all_gather x1, waiting for transfers between devices, local(): w_panel = lax.all_gather(small_weight, 'col', axis=1, tiled=True)  53.3 us
    all_gather x1, waiting for transfers between devices, local(): delta_all = lax.all_gather(delta_local, 'row', axis=0, tiled=True)  48.2 us
    unnamed x10, waiting for transfers between devices  48.1 us
    reduce_scatter x1, waiting for transfers between devices, local(): lax.psum_scatter(contract(block, grad_grown, 0, 0), 'row', scatter_dimens...  44.5 us
  transfers between devices with their start and end apart: 9, of which 8 were waited for; matrix products, arithmetic and copies ran while one was open for 4% of the time, Pallas kernels for 0%

commit v1 on v0

v1 whole, which is shorter than its diff:
```python
import functools

import jax
import jax.numpy as jnp
from jax import lax
from jax.experimental import pallas as pl
from jax.experimental.pallas import tpu as pltpu
from jax.sharding import PartitionSpec as P

MESH = pl.DeviceIdType.MESH
F32 = jnp.float32
BF16 = jnp.bfloat16
HW = 176
HP = 128
FP = 224
HA = 160
NSEM = 128
KT = (0, 2, 1, 3)


def nn(a, b):
    return jnp.dot(a, b, preferred_element_type=F32)


def nt(a, b):
    return lax.dot_general(a, b, (((1,), (1,)), ((), ())), preferred_element_type=F32)


def lanes(start, size):
    return pl.ds(pl.multiple_of(start, 128), size)


def rows(start, size):
    return pl.ds(pl.multiple_of(start, 16), size)


def kernel(
    scale,
    act, cot, w, a, b,
    gr_out, gc_out, gs_out,
    wpad, wsend, wbuf, aown, ax, abuf, bp, bpt, actp, att,
    ps, prcv, pblk, pbuf,
    cs, crcv, ct, delta, dt,
    bs, brcv, bt,
    qs, qc, qo, qh, qry, qzf, qzs, qrz, qfin, qt,
    gs, gc, go, gh, gry, gzf, gzs, grz, gfin, gst,
    hs, hc, ho, hh, hry, hzf, hzs, hrz, hfin, hp,
    ssem, rsem, lsem,
):
    r = lax.axis_index("row")
    c = lax.axis_index("col")
    x, zlo = r // 2, r % 2
    zhi, y, core = c // 8, (c // 2) % 4, c % 2
    yh, yl = y // 2, y % 2
    kt = 2 * core + yl
    far = 1 - core

    def row_peer(d):
        return ((r + d) % 8, c)

    def y_peer(d):
        return (r, zhi * 8 + ((y + d) % 4) * 2 + core)

    def z_peer(d):
        return (r, ((zhi + d) % 4) * 8 + y * 2 + core)

    core_peer = (r, c + 1 - 2 * core)
    t_peer = (zhi * 2 + yh, x * 8 + zlo * 4 + yl * 2 + core)
    stays = jnp.logical_and(x == zhi, zlo == yh)
    moves = jnp.logical_not(stays)

    used = [0]
    sent = []

    def push(src, dst, device):
        i = used[0]
        used[0] += 1
        copy = pltpu.make_async_remote_copy(
            src_ref=src, dst_ref=dst, send_sem=ssem.at[i], recv_sem=rsem.at[i],
            device_id=device, device_id_type=MESH,
        )
        copy.start()
        sent.append(copy)
        return copy

    swaps = []

    def swap(src, dst):
        i = used[0]
        used[0] += 1
        remote = pltpu.make_async_remote_copy(
            src_ref=src, dst_ref=dst, send_sem=ssem.at[i], recv_sem=rsem.at[i],
            device_id=t_peer, device_id_type=MESH,
        )
        local = pltpu.make_async_copy(src, dst, lsem.at[len(swaps)])

        @pl.when(moves)
        def _():
            remote.start()

        @pl.when(stays)
        def _():
            local.start()

        swaps.append(remote)

        def wait():
            @pl.when(moves)
            def _():
                remote.wait_recv()

            @pl.when(stays)
            def _():
                local.wait()

        return wait

    barrier = pltpu.get_barrier_semaphore()
    for d in range(1, 8):
        pl.semaphore_signal(barrier, inc=1, device_id=row_peer(d), device_id_type=MESH)
    for d in range(1, 4):
        pl.semaphore_signal(barrier, inc=1, device_id=y_peer(d), device_id_type=MESH)
        pl.semaphore_signal(barrier, inc=1, device_id=z_peer(d), device_id_type=MESH)
    pl.semaphore_signal(barrier, inc=1, device_id=core_peer, device_id_type=MESH)

    @pl.when(moves)
    def _():
        pl.semaphore_signal(barrier, inc=1, device_id=t_peer, device_id_type=MESH)

    aown[:, 0:64] = a[...]
    aown[:, 64:128] = a[...]
    wpad[...] = jnp.zeros_like(wpad)
    wpad[:, 0:172] = w[...]
    wsend[...] = wpad[...].T[0:HW]

    @pl.when(moves)
    def _():
        pl.semaphore_wait(barrier, 15)

    @pl.when(stays)
    def _():
        pl.semaphore_wait(barrier, 14)

    slot = lanes(1024 * yh + 256 * zhi, 256)
    band = lanes(1024 * yh, 1024)
    t_slot = lanes(1024 * zlo + 256 * x, 256)
    wrow = rows(HW * kt, HW)
    prow = rows(HP * kt, HP)

    a_pair = push(aown.at[rows(HA * far, HA), :], ax, core_peer)
    w_swap = swap(wsend, wbuf.at[wrow, t_slot])

    a_pair.wait_recv()
    lane = lax.broadcasted_iota(jnp.int32, (HA, 128), 1)
    arow = rows(HA * core, HA)
    abuf[y, arow, lanes(128 * zhi, 128)] = jnp.where(lane // 64 == core, aown[arow, :], ax[...])

    def gather_z(block):
        return [push(block, block, z_peer(d)) for d in (1, 2, 3)]

    def gather_y(block):
        return [push(block, block, y_peer(d)) for d in (1, 2, 3)]

    def wait_all(copies):
        for copy in copies:
            copy.wait_recv()

    a_z = gather_z(abuf.at[y, arow, lanes(128 * zhi, 128)])
    w_swap()
    w_z = gather_z(wbuf.at[wrow, slot])

    wait_all(a_z)
    a_y = gather_y(abuf.at[y, arow, :])
    a_core = [push(abuf.at[y, arow, :], abuf.at[y, arow, :], core_peer)]
    wait_all(w_z)
    w_y = gather_y(wbuf.at[wrow, band])
    w_core = [push(wbuf.at[wrow, band], wbuf.at[wrow, band], core_peer)]

    bp[...] = jnp.zeros_like(bp)
    for k in range(4):
        bp[0:216, HW * KT[k]:HW * KT[k] + 172] = b[:, 172 * k:172 * k + 172]
    bpt[...] = bp[...].T

    for d in (1, 2, 3):
        a_y[d - 1].wait_recv()
        block = abuf.at[(y + 4 - d) % 4, arow, :]
        a_core.append(push(block, block, core_peer))
    wait_all(a_core)

    for q in range(4):
        part = nn(act[...], abuf[q]).astype(BF16)
        for z in range(4):
            ps[2 * z + q // 2, :, 128 * (q % 2):128 * (q % 2) + 128] = part[:, 128 * z:128 * z + 128]
    p_rs = [push(ps.at[(r + d) % 8], prcv.at[d - 1], row_peer(d)) for d in range(1, 8)]

    for d in (1, 2, 3):
        w_y[d - 1].wait_recv()
        other = (y + 4 - d) % 4
        block = wbuf.at[rows(HW * (2 * core + other % 2), HW), lanes(1024 * (other // 2), 1024)]
        w_core.append(push(block, block, core_peer))

    wait_all(p_rs)
    total = ps[r].astype(F32)
    for d in range(7):
        total = total + prcv[d].astype(F32)
    pblk[...] = total.astype(BF16)
    p_swap = swap(pblk, pbuf.at[prow, t_slot])

    wait_all(w_core)
    c_rs = []
    for d in range(1, 8):
        peer = (r + d) % 8
        cs[d - 1] = nn(bp[0:FP, 0:4 * HW], wbuf[:, lanes(1024 * (peer % 2) + 256 * (peer // 2), 256)]).astype(BF16)
        c_rs.append(push(cs.at[d - 1], crcv.at[d - 1], row_peer(d)))
    own = lanes(1024 * zlo + 256 * x, 256)
    total = nn(bp[0:FP, 0:4 * HW], wbuf[:, own])

    p_swap()
    p_z = gather_z(pbuf.at[prow, slot])

    for d in range(7):
        c_rs[d].wait_recv()
        total = total + crcv[d].astype(F32)
    ct[:, own] = total.astype(BF16)
    c_ag = [push(ct.at[:, own], ct.at[:, own], row_peer(d)) for d in range(1, 8)]

    wait_all(p_z)
    p_y = gather_y(pbuf.at[prow, band])
    p_core = [push(pbuf.at[prow, band], pbuf.at[prow, band], core_peer)]
    delta[...] = jnp.zeros_like(delta)
    actp[...] = jnp.zeros_like(actp)
    actp[:, 0:320] = act[...]
    att[...] = actp[...].T
    for d in (1, 2, 3):
        p_y[d - 1].wait_recv()
        other = (y + 4 - d) % 4
        block = pbuf.at[rows(HP * (2 * core + other % 2), HP), lanes(1024 * (other // 2), 1024)]
        p_core.append(push(block, block, core_peer))
    wait_all(p_core)
    wait_all(c_ag)

    for k in range(4):
        t = KT[k]
        hidden = nt(pbuf[HP * t:HP * t + HP, :], ct[...])[:, 0:216]
        s = 1.0 / (1.0 + jnp.exp(-hidden))
        grad = cot[HP * k:HP * k + HP, :].astype(F32) * s * (1.0 + hidden * (1.0 - s))
        delta[HP * t:HP * t + HP, 0:216] = grad.astype(BF16)
    dt[...] = delta[...].T

    b_rs = []
    for d in range(1, 8):
        peer = (r + d) % 8
        bs[d - 1] = nn(dt[0:FP, :], pbuf[:, lanes(1024 * (peer % 2) + 256 * (peer // 2), 256)]).astype(BF16)
        b_rs.append(push(bs.at[d - 1], brcv.at[d - 1], row_peer(d)))

    def tiles(body):
        lax.fori_loop(0, 8, lambda i, _: (body(lanes(256 * i, 256)), 0)[1], 0)

    def q_far(at):
        qs[:, at] = nn(delta[rows(2 * HP * far, 2 * HP), 0:FP], ct[:, at]).astype(BF16)

    def q_own(at):
        qo[:, at] = nn(delta[rows(2 * HP * core, 2 * HP), 0:FP], ct[:, at])

    tiles(q_far)
    q_core = push(qs, qc, core_peer)
    tiles(q_own)
    total = nn(dt[0:FP, :], pbuf[:, own])
    q_core.wait_recv()

    def q_sum(at):
        value = qo[:, at] + qc[:, at].astype(F32)
        qo[:, at] = value
        qh[:, at] = value.astype(BF16)

    tiles(q_sum)

    def scatter_y(half, height, into):
        copies = []
        for d in (1, 2, 3):
            other = (y + d) % 4
            copies.append(push(
                half.at[rows(height * (other % 2), height), lanes(1024 * (other // 2), 1024)],
                into.at[d - 1], y_peer(d)))
        return copies

    def scatter_z(part, width, into):
        return [
            push(part.at[:, lanes(width * ((zhi + d) % 4), width)], into.at[d - 1], z_peer(d))
            for d in (1, 2, 3)
        ]

    q_y = scatter_y(qh, HP, qry)

    for d in range(7):
        b_rs[d].wait_recv()
        total = total + brcv[d].astype(F32)
    bt[:, own] = (total * scale).astype(BF16)
    b_ag = [push(bt.at[:, own], bt.at[:, own], row_peer(d)) for d in range(1, 8)]

    def sum_y(copies, full, height, received, wide, narrow):
        wait_all(copies)
        for z in range(4):
            at = slice(256 * z, 256 * z + 256)
            value = full[rows(height * yl, height), lanes(1024 * yh + 256 * z, 256)]
            for d in range(3):
                value = value + received[d, :, at].astype(F32)
            wide[:, at] = value
            narrow[:, at] = value.astype(BF16)

    def sum_z(copies, wide, width, received):
        wait_all(copies)
        value = wide[:, lanes(width * zhi, width)]
        for d in range(3):
            value = value + received[d].astype(F32)
        return value

    sum_y(q_y, qo, HP, qry, qzf, qzs)
    q_z = scatter_z(qzs, 256, qrz)
    qfin[...] = (sum_z(q_z, qzf, 256, qrz) * scale).astype(BF16)
    q_swap = swap(qfin, qt.at[:, slot])

    wait_all(b_ag)

    def g_far(at):
        gs[:, at] = nn(bpt[rows(2 * HW * far, 2 * HW), 0:FP], bt[:, at]).astype(BF16)

    def g_own(at):
        go[:, at] = nn(bpt[rows(2 * HW * core, 2 * HW), 0:FP], bt[:, at])

    tiles(g_far)
    g_core = push(gs, gc, core_peer)
    q_swap()
    q_ag = [push(qt.at[:, own], qt.at[:, own], row_peer(d)) for d in range(1, 8)]
    tiles(g_own)
    g_core.wait_recv()

    def g_sum(at):
        value = go[:, at] + gc[:, at].astype(F32)
        go[:, at] = value
        gh[:, at] = value.astype(BF16)

    tiles(g_sum)
    g_y = scatter_y(gh, HW, gry)

    for t in range(4):
        gc_out[:, HW * t:HW * t + HW] = nt(bt[...], wbuf[HW * t:HW * t + HW, :]).astype(BF16)

    wait_all(q_ag)
    for q in range(8):
        part = nn(att[rows(HA * far, HA), :], qt[:, 256 * q:256 * q + 256]).astype(BF16)
        for v in range(2):
            hs[2 * (q // 4) + v, :, 128 * (q % 4):128 * (q % 4) + 128] = part[:, 128 * v:128 * v + 128]
    h_core = push(hs, hc, core_peer)
    for q in range(8):
        part = nn(att[arow, :], qt[:, 256 * q:256 * q + 256])
        for v in range(2):
            ho[2 * (q // 4) + v, :, 128 * (q % 4):128 * (q % 4) + 128] = part[:, 128 * v:128 * v + 128]
    h_core.wait_recv()
    for q in range(4):
        value = ho[q] + hc[q].astype(F32)
        ho[q] = value
        hh[q] = value.astype(BF16)
    h_y = [push(hh.at[(y + d) % 4], hry.at[d - 1], y_peer(d)) for d in (1, 2, 3)]

    sum_y(g_y, go, HW, gry, gzf, gzs)
    g_z = scatter_z(gzs, 256, grz)

    wait_all(h_y)
    value = ho[y]
    for d in range(3):
        value = value + hry[d].astype(F32)
    hzf[...] = value
    hzs[...] = value.astype(BF16)
    h_z = scatter_z(hzs, 128, hrz)

    gfin[...] = sum_z(g_z, gzf, 256, grz).astype(BF16)
    g_swap = swap(gfin, gst.at[0:HW, :])

    hfin[...] = sum_z(h_z, hzf, 128, hrz).astype(BF16)
    h_pair = push(hfin, hp, core_peer)
    first = core == 0
    gr_out[arow, :] = jnp.where(first, hfin[:, 0:64], hfin[:, 64:128])
    h_pair.wait_recv()
    gr_out[rows(HA * far, HA), :] = jnp.where(first, hp[:, 0:64], hp[:, 64:128])

    g_swap()
    gst[HW:256, :] = jnp.zeros((256 - HW, 256), BF16)
    gs_out[...] = gst[...].T[:, 0:172]

    for copy in sent:
        copy.wait_send()
    for remote in swaps:
        @pl.when(moves)
        def _():
            remote.wait_send()


def local(activations, cotangent, small_weight, grow_rows, grow_cols):
    scale = float(32 * activations.shape[0]) ** -0.5
    bf, f32 = (lambda *s: pltpu.VMEM(s, BF16)), (lambda *s: pltpu.VMEM(s, F32))
    scratch = [
        bf(256, 256), bf(HW, 256), bf(4 * HW, 2048), bf(320, 128), bf(HA, 128), bf(4, 320, 512),
        bf(256, 768), bf(768, 256), bf(128, 384), bf(384, 128),
        bf(8, 128, 256), bf(7, 128, 256), bf(128, 256), bf(512, 2048),
        bf(7, FP, 256), bf(7, FP, 256), bf(FP, 2048), bf(512, 256), bf(256, 512),
        bf(7, FP, 256), bf(7, FP, 256), bf(FP, 2048),
        bf(256, 2048), bf(256, 2048), f32(256, 2048), bf(256, 2048), bf(3, HP, 1024),
        f32(HP, 1024), bf(HP, 1024), bf(3, HP, 256), bf(HP, 256), bf(HP, 2048),
        bf(2 * HW, 2048), bf(2 * HW, 2048), f32(2 * HW, 2048), bf(2 * HW, 2048), bf(3, HW, 1024),
        f32(HW, 1024), bf(HW, 1024), bf(3, HW, 256), bf(HW, 256), bf(256, 256),
        bf(4, HA, 512), bf(4, HA, 512), f32(4, HA, 512), bf(4, HA, 512), bf(3, HA, 512),
        f32(HA, 512), bf(HA, 512), bf(3, HA, 128), bf(HA, 128), bf(HA, 128),
        pltpu.SemaphoreType.DMA((NSEM,)), pltpu.SemaphoreType.DMA((NSEM,)), pltpu.SemaphoreType.DMA((4,)),
    ]
    vmem = pl.BlockSpec(memory_space=pltpu.VMEM)
    gr, gc, gs = pl.pallas_call(
        functools.partial(kernel, scale),
        out_shape=(
            jax.ShapeDtypeStruct((320, 64), BF16),
            jax.ShapeDtypeStruct((FP, 4 * HW), BF16),
            jax.ShapeDtypeStruct((256, 172), BF16),
        ),
        in_specs=[vmem] * 5,
        out_specs=(vmem,) * 3,
        scratch_shapes=scratch,
        compiler_params=pltpu.CompilerParams(
            collective_id=0, has_side_effects=True, vmem_limit_bytes=56 * 2**20
        ),
        cost_estimate=pl.CostEstimate(flops=3_700_000_000, bytes_accessed=3_000_000, transcendentals=110_592),
        name="grow",
    )(activations, cotangent, small_weight, grow_rows, grow_cols)
    gc = jnp.concatenate([gc[0:216, HW * KT[k]:HW * KT[k] + 172] for k in range(4)], axis=1)
    return gr, gc, gs


def solution(mesh):
    return jax.shard_map(
        local,
        mesh=mesh,
        in_specs=(
            P("col", "row"),
            P("row", "col"),
            P("row", "col"),
            P("row", "col"),
            P("col", "row"),
        ),
        out_specs=(P("row", "col"), P("col", "row"), P("row", "col")),
        check_vma=False,
    )
```

time: 734 us -> 185 us (0.25)
  waiting for transfers between devices: 415 us -> 0 us
  blocking collectives: 250 us -> 0 us
  Pallas kernels: 0 us -> 175 us
  matrix products: 25.7 us -> 0 us
  between operations: 14.6 us -> 0.67 us
  local copies, waits for them, and re-layouts: 19.5 us -> 8.28 us
    all_gather x5 -> x0, waiting for transfers between devices: 243 us -> none  [the longest x1 65.7 us: local(): b_panel = lax.all_gather(grow_cols, 'row', axis=1, tiled=True)]
    unnamed x1 -> x0, blocking collectives: 222 us -> none
    pallas_call x0 -> x1, Pallas kernels: none -> 175 us  [local(): pl.pallas_call(functools.partial(kernel, scale), out_shape=(jax.ShapeDtyp...]
    reduce_scatter x3 -> x0, waiting for transfers between devices: 124 us -> none  [the longest x1 79.9 us: local(): lax.psum_scatter(jnp.dot(block, grown_panel, preferred_element_type=jnp.f...]
    unnamed x10 -> x0, waiting for transfers between devices: 48.1 us -> none
    all_gather x1 -> x0, blocking collectives: 28.9 us -> none  [local(): c_panel = lax.all_gather(product, 'row', axis=0, tiled=True)]
    dot_general x7 -> x0, matrix products: 25.7 us -> none  [the longest x6 19.1 us: contract(): lax.dot_general(left, right, (((left_dim,), (right_dim,)), ((), ())), pre...]
    unnamed x16 -> x12, local copies, waits for them, and re-layouts: 17.1 us -> 8.11 us
  transfers between devices with their start and end apart: 9 -> 0, of which waited for: 8 -> 0; matrix products, arithmetic and copies ran while one was open for 4% -> 0% of each run, Pallas kernels for 0% -> 0%
where the time goes in v1:
time: 185 us
  Pallas kernels  175 us (95%)
  local copies, waits for them, and re-layouts  8.28 us (4%)
    pallas_call x1, Pallas kernels, local(): pl.pallas_call(functools.partial(kernel, scale), out_shape=(jax.ShapeDtyp...  175 us
    unnamed x12, local copies, waits for them, and re-layouts  8.11 us

profile of v1, /device:TPU:33, one launch (start us, length us, event | category | flops | bytes accessed | tf_op | source)
XLA Modules:
  0.0 184.6 jit_solution(6688254158604692394)
XLA Ops:
  0.6 0.0 copy-start.2
  0.6 1.6 copy.11.a
  2.2 0.0 copy-start.1
  2.2 1.7 copy.8.act
  3.9 0.0 copy-done.2
  3.9 0.7 copy.10.w
  4.6 0.0 copy-done.1
  4.6 0.8 copy.9.cot
  5.5 174.7 %grow.1 = (bf16[320,64]{1,0:T(8,128)(2,1)}, bf16[224,704]{1,0:T(8,128)(2,1)}, bf16[256,172]{1,0:T(8,128)(2,1)}) custom-call(bf16[128,320]{1,0:T(8,128)(2,1)} %copy.8.act, bf16[512,216]{1,0:T(8,128)(2,1)} %copy.9.cot, bf16[256,172]{1,0:T(8,128)(2,1)} %copy.10.w, bf16[320,64]{1,0:T(8,128)(2,1)} %copy.11.a, bf16[216,688]{1,0:T(8,128)(2,1)} %b.1), custom_call_target="tpu_custom_call" | custom-call | flops 3700000000 | bytes 3000000 | tf_op jit(solution)/shard_map/grow/pallas_call | solution.py:417
  180.2 0.0 copy-start
  180.2 1.6 copy.12
  181.8 1.6 copy.13
  183.5 0.0 copy-done
  183.5 0.2 fusion
  183.7 0.9 pad_maximum_fusion
Async XLA Ops:
  0.6 3.2 %copy-start.2 = (bf16[256,172]{0,1:T(8,128)(2,1)S(1)}, bf16[256,172]{0,1:T(8,128)(2,1)}, u32[]{:S(2)}) copy-start(bf16[256,172]{0,1:T(8,128)(2,1)} %param.7) | copy-start | bytes 264196
  2.2 2.4 %copy-start.1 = (bf16[512,216]{0,1:T(8,128)(2,1)S(1)}, bf16[512,216]{0,1:T(8,128)(2,1)}, u32[]{:S(2)}) copy-start(bf16[512,216]{0,1:T(8,128)(2,1)} %param.6) | copy-start | bytes 663556
  180.2 3.3 %copy-start = (bf16[224,704]{1,0:T(8,128)(2,1)S(1)}, bf16[224,704]{1,0:T(8,128)(2,1)}, u32[]{:S(2)}) copy-start(bf16[224,704]{1,0:T(8,128)(2,1)} %get-tuple-element.7) | copy-start | bytes 946180

commit v2 on v0

v2 whole, which is shorter than its diff:
```python
import functools

import jax
import jax.numpy as jnp
from jax import lax
from jax.experimental import pallas as pl
from jax.experimental.pallas import tpu as pltpu
from jax.sharding import PartitionSpec as P

MESH = pl.DeviceIdType.MESH
F32 = jnp.float32
BF16 = jnp.bfloat16
HW = 176
HP = 128
FP = 224
LA = 384
NSEM = 256
KT = (0, 2, 1, 3)
CW = ((0, 96), (96, 80))
CP = ((0, 64), (64, 64))
CQ = ((0, 64), (64, 64))


def nn(a, b):
    return jnp.dot(a, b, preferred_element_type=F32)


def nt(a, b):
    return lax.dot_general(a, b, (((1,), (1,)), ((), ())), preferred_element_type=F32)


def lanes(start, size):
    return pl.ds(pl.multiple_of(start, 128), size)


def rows(start, size):
    return pl.ds(pl.multiple_of(start, 16), size)


def kernel(
    scale,
    act, cot, w, a, b,
    gr_out, gc_out, gs_out,
    wsend, wbuf, abuf, bp, bpt, actp, actt,
    ps, prcv, pblk, pbuf,
    cs, crcv, ct, delta, dt,
    bs, brcv, bt,
    qfar, qgot, qown, qhalf, qry, qyf, qys, qrx, qrz, qfin, qt,
    gfar, ggot, gown, ghalf, gry, gyf, gys, grx, grz,
    hfull, hs, hc, ho, hh, hry, hzf, hzs, hrz,
    ssem, rsem,
):
    r = lax.axis_index("row")
    c = lax.axis_index("col")
    x, zlo = r // 2, r % 2
    zhi, y, core = c // 8, (c // 2) % 4, c % 2
    yh, yl = y // 2, y % 2
    kt = 2 * core + yl
    far = 1 - core
    diag = zlo == yh
    stays = jnp.logical_and(x == zhi, diag)

    def row_peer(d):
        return ((r + d) % 8, c)

    def y_peer(d):
        return (r, zhi * 8 + ((y + d) % 4) * 2 + core)

    def z_peer(d):
        return (r, ((zhi + d) % 4) * 8 + y * 2 + core)

    core_peer = (r, c + 1 - 2 * core)

    def swap_target(j):
        return (zhi * 2 + yh, j * 8 + zlo * 4 + yl * 2 + core)

    def swap_source(s):
        return (s * 2 + yh, x * 8 + zlo * 4 + yl * 2 + core)

    def turn_peer(j):
        return (x * 2 + yh, j * 8 + zlo * 4 + yl * 2 + core)

    used = [0]
    sent = []

    def push(src, dst, device):
        i = used[0]
        used[0] += 1
        copy = pltpu.make_async_remote_copy(
            src_ref=src, dst_ref=dst, send_sem=ssem.at[i], recv_sem=rsem.at[i],
            device_id=device, device_id_type=MESH,
        )
        copy.start()
        sent.append((copy, None))
        return copy

    def push_when(cond, src, dst, device):
        i = used[0]
        used[0] += 1
        copy = pltpu.make_async_remote_copy(
            src_ref=src, dst_ref=dst, send_sem=ssem.at[i], recv_sem=rsem.at[i],
            device_id=device, device_id_type=MESH,
        )

        @pl.when(cond)
        def _():
            copy.start()

        sent.append((copy, cond))
        return copy

    def wait_all(copies):
        for copy in copies:
            copy.wait_recv()

    barrier = pltpu.get_barrier_semaphore()

    def greet(device):
        pl.semaphore_signal(barrier, inc=1, device_id=device, device_id_type=MESH)

    for d in range(1, 8):
        greet(row_peer(d))
    for d in range(1, 4):
        greet(y_peer(d))
        greet(z_peer(d))
    greet(core_peer)
    for s in range(4):
        pl.when(jnp.logical_not(jnp.logical_and(stays, x == s)))(lambda s=s: greet(swap_source(s)))
    for d in range(1, 4):
        greet(turn_peer((zhi + d) % 4))
    pl.when(jnp.logical_not(diag))(lambda: greet(turn_peer(zhi)))

    wsend[0:172, :] = w[...]
    wsend[172:HW, :] = jnp.zeros((HW - 172, 256), BF16)
    acol = rows(64 * (2 * yl + core), 64)
    abuf[yh, 0, acol, 0:320] = a[...]
    abuf[yh, 0, acol, 320:LA] = jnp.zeros((64, LA - 320), BF16)

    @pl.when(stays)
    def _():
        pl.semaphore_wait(barrier, 20)

    @pl.when(jnp.logical_and(diag, x != zhi))
    def _():
        pl.semaphore_wait(barrier, 21)

    @pl.when(jnp.logical_not(diag))
    def _():
        pl.semaphore_wait(barrier, 22)

    t_slot = lanes(1024 * zlo + 256 * x, 256)
    band = lanes(1024 * yh, 1024)

    def swap_gather(src, buf, height, chunk):
        off, size = chunk
        base = used[0]
        used[0] += 4
        at = rows(height * kt + off, size)
        for d in range(4):
            copy = pltpu.make_async_remote_copy(
                src_ref=src.at[off:off + size, :], dst_ref=buf.at[at, t_slot],
                send_sem=ssem.at[base + d], recv_sem=rsem.at[base + x],
                device_id=swap_target((zhi + d) % 4), device_id_type=MESH,
            )
            if d:
                copy.start()
                sent.append((copy, None))
            else:
                pl.when(jnp.logical_not(stays))(copy.start)
                sent.append((copy, jnp.logical_not(stays)))

        @pl.when(stays)
        def _():
            buf[at, t_slot] = src[off:off + size, :]

        def wait():
            for s in range(4):
                copy = pltpu.make_async_remote_copy(
                    src_ref=src.at[off:off + size, :], dst_ref=buf.at[at, t_slot],
                    send_sem=ssem.at[base], recv_sem=rsem.at[base + s],
                    device_id=core_peer, device_id_type=MESH,
                )
                pl.when(jnp.logical_not(jnp.logical_and(stays, x == s)))(copy.wait_recv)

        return wait

    def band_y(buf, height, chunk):
        off, size = chunk
        block = buf.at[rows(height * kt + off, size), band]
        return [push(block, block, y_peer(d)) for d in (1, 2, 3)]

    def band_core(buf, height, d):
        other = (y + 4 - d) % 4
        block = buf.at[rows(height * (2 * core + other % 2), height), lanes(1024 * (other // 2), 1024)]
        return push(block, block, core_peer)

    first = abuf.at[yh, 0, acol, :]
    a_z = [push(first, abuf.at[yh, 4 - d, acol, :], z_peer(d)) for d in (1, 2, 3)]
    a_y = [push(first, first, y_peer(d)) for d in (1, 2, 3)]
    w_sw = [swap_gather(wsend, wbuf, HW, chunk) for chunk in CW]
    a_core = [push(first, first, core_peer)]

    bp[...] = jnp.zeros_like(bp)
    for k in range(4):
        bp[0:216, HW * KT[k]:HW * KT[k] + 172] = b[:, 172 * k:172 * k + 172]
    actt[0:320, :] = act[...]
    actt[320:LA, :] = jnp.zeros((LA - 320, 128), BF16)
    actp[...] = actt[...].T

    wait_all(a_z)
    rest = abuf.at[yh, 1:4, acol, :]
    a_y2 = [push(rest, rest, y_peer(d)) for d in (1, 2, 3)]
    a_core.append(push(rest, rest, core_peer))

    w_sw[0]()
    w_y = [band_y(wbuf, HW, CW[0])]
    bpt[...] = bp[...].T

    for d in (1, 2, 3):
        a_y[d - 1].wait_recv()
        a_y2[d - 1].wait_recv()
        other = (y + 4 - d) % 4
        block = abuf.at[other // 2, :, rows(64 * (2 * (other % 2) + core), 64), :]
        a_core.append(push(block, block, core_peer))

    w_sw[1]()
    w_y.append(band_y(wbuf, HW, CW[1]))
    w_core = [band_core(wbuf, HW, 0)]
    wait_all(a_core)

    def p_term(peer):
        return nt(actp[...], abuf[peer % 2, (peer // 2 + 4 - zhi) % 4])

    p_rs = []
    for d in range(1, 8):
        ps[d - 1] = p_term((r + d) % 8).astype(BF16)
        p_rs.append(push(ps.at[d - 1], prcv.at[d - 1], row_peer(d)))
    total = p_term(r)
    dt[...] = jnp.zeros_like(dt)

    for d in (1, 2, 3):
        w_y[0][d - 1].wait_recv()
        w_y[1][d - 1].wait_recv()
        w_core.append(band_core(wbuf, HW, d))

    for d in range(7):
        p_rs[d].wait_recv()
        total = total + prcv[d].astype(F32)
    pblk[...] = total.astype(BF16)
    p_sw = [swap_gather(pblk, pbuf, HP, chunk) for chunk in CP]

    wait_all(w_core)

    def panel(peer):
        return lanes(1024 * (peer % 2) + 256 * (peer // 2), 256)

    own = panel(r)
    c_rs = []
    for d in range(1, 8):
        cs[d - 1] = nn(bp[0:FP, 0:4 * HW], wbuf[:, panel((r + d) % 8)]).astype(BF16)
        c_rs.append(push(cs.at[d - 1], crcv.at[d - 1], row_peer(d)))
    total = nn(bp[0:FP, 0:4 * HW], wbuf[:, own])

    p_sw[0]()
    p_y = [band_y(pbuf, HP, CP[0])]
    p_sw[1]()
    p_y.append(band_y(pbuf, HP, CP[1]))
    p_core = [band_core(pbuf, HP, 0)]

    for d in range(7):
        c_rs[d].wait_recv()
        total = total + crcv[d].astype(F32)
    ct[:, own] = total.astype(BF16)
    c_ag = [push(ct.at[:, own], ct.at[:, own], row_peer(d)) for d in range(1, 8)]

    for d in (1, 2, 3):
        p_y[0][d - 1].wait_recv()
        p_y[1][d - 1].wait_recv()
        p_core.append(band_core(pbuf, HP, d))
    wait_all(p_core)
    wait_all(c_ag)

    for k in range(4):
        t = KT[k]
        hidden = nt(ct[...], pbuf[HP * t:HP * t + HP, :])[0:216, :]
        s = 1.0 / (1.0 + jnp.exp(-hidden))
        grad = cot[:, HP * k:HP * k + HP].astype(F32) * s * (1.0 + hidden * (1.0 - s))
        dt[0:216, HP * t:HP * t + HP] = grad.astype(BF16)

    b_rs = []
    for d in range(1, 8):
        bs[d - 1] = nn(dt[0:FP, :], pbuf[:, panel((r + d) % 8)]).astype(BF16)
        b_rs.append(push(bs.at[d - 1], brcv.at[d - 1], row_peer(d)))
    delta[...] = dt[...].T

    def tiles(body):
        lax.fori_loop(0, 8, lambda i, _: (body(lanes(256 * i, 256)), 0)[1], 0)

    class Scatter:
        def __init__(self, height, chunks, far_ref, got, own_ref, half, ry, yf, ys, rx, rz):
            self.height, self.chunks = height, chunks
            self.far, self.got, self.own, self.half = far_ref, got, own_ref, half
            self.ry, self.yf, self.ys, self.rx, self.rz = ry, yf, ys, rx, rz
            n = len(chunks)
            self.core, self.y, self.x, self.z = [None] * n, [None] * n, [None] * n, [None] * n

        def to_core(self, i):
            off, size = self.chunks[i]
            self.core[i] = []
            for v in range(2):
                at = slice(self.height * v + off, self.height * v + off + size)
                self.core[i].append(push(self.far.at[at, :], self.got.at[at, :], core_peer))

        def to_y(self, i):
            off, size = self.chunks[i]
            wait_all(self.core[i])

            def add(at):
                for v in range(2):
                    part = slice(self.height * v + off, self.height * v + off + size)
                    value = self.own[part, at] + self.got[part, at].astype(F32)
                    self.own[part, at] = value
                    self.half[part, at] = value.astype(BF16)

            tiles(add)
            self.y[i] = []
            for d in (1, 2, 3):
                other = (y + d) % 4
                self.y[i].append(push(
                    self.half.at[rows(self.height * (other % 2) + off, size), lanes(1024 * (other // 2), 1024)],
                    self.ry.at[d - 1, off:off + size, :], y_peer(d)))

        def to_x(self, i):
            off, size = self.chunks[i]
            wait_all(self.y[i])
            for q in range(4):
                at = slice(256 * q, 256 * q + 256)
                value = self.own[rows(self.height * yl + off, size), lanes(1024 * yh + 256 * q, 256)]
                for d in range(3):
                    value = value + self.ry[d, off:off + size, at].astype(F32)
                self.ys[off:off + size, at] = value.astype(BF16)
            self.x[i] = [
                push(self.ys.at[off:off + size, lanes(256 * ((x + d) % 4), 256)],
                     self.rx.at[x, off:off + size, :], row_peer(2 * d))
                for d in (1, 2, 3)
            ]
            self.rx[x, off:off + size, :] = self.ys[off:off + size, lanes(256 * x, 256)]

        def to_z(self, i):
            off, size = self.chunks[i]
            wait_all(self.x[i])
            self.z[i] = [
                push(self.rx.at[(zhi + d) % 4, off:off + size, :], self.rz.at[zhi, off:off + size, :],
                     turn_peer((zhi + d) % 4))
                for d in (1, 2, 3)
            ]
            self.last = push_when(
                jnp.logical_not(diag), self.rx.at[zhi, off:off + size, :], self.rz.at[zhi, off:off + size, :],
                turn_peer(zhi))
            self.z[i].append(self.last)

            @pl.when(diag)
            def _():
                self.rz[zhi, off:off + size, :] = self.rx[zhi, off:off + size, :]

        def result(self, i):
            off, size = self.chunks[i]
            wait_all(self.z[i][:3])
            pl.when(jnp.logical_not(diag))(self.z[i][3].wait_recv)
            value = self.rz[0, off:off + size, :].astype(F32)
            for s in range(1, 4):
                value = value + self.rz[s, off:off + size, :].astype(F32)
            return value

    q = Scatter(HP, CQ, qfar, qgot, qown, qhalf, qry, qyf, qys, qrx, qrz)

    def q_far(at):
        qfar[:, at] = nn(delta[rows(2 * HP * far, 2 * HP), 0:FP], ct[:, at]).astype(BF16)

    def q_own(at):
        qown[:, at] = nn(delta[rows(2 * HP * core, 2 * HP), 0:FP], ct[:, at])

    tiles(q_far)
    q.to_core(0)
    q.to_core(1)
    tiles(q_own)
    total = nn(dt[0:FP, :], pbuf[:, own])
    q.to_y(0)
    q.to_y(1)

    for d in range(7):
        b_rs[d].wait_recv()
        total = total + brcv[d].astype(F32)
    bt[:, own] = (total * scale).astype(BF16)
    b_ag = [push(bt.at[:, own], bt.at[:, own], row_peer(d)) for d in range(1, 8)]

    q.to_x(0)
    q.to_x(1)
    q.to_z(0)

    g = Scatter(HW, CW, gfar, ggot, gown, ghalf, gry, gyf, gys, grx, grz)
    wait_all(b_ag)

    def g_far(at):
        gfar[:, at] = nn(bpt[rows(2 * HW * far, 2 * HW), 0:FP], bt[:, at]).astype(BF16)

    def g_own(at):
        gown[:, at] = nn(bpt[rows(2 * HW * core, 2 * HW), 0:FP], bt[:, at])

    tiles(g_far)
    g.to_core(0)
    g.to_core(1)
    q.to_z(1)
    tiles(g_own)
    g.to_y(0)
    g.to_y(1)

    for i, (off, size) in enumerate(CQ):
        qfin[off:off + size, :] = (q.result(i) * scale).astype(BF16)
    qt[:, own] = qfin[...]
    q_ag = [push(qfin, qt.at[:, own], row_peer(d)) for d in range(1, 8)]

    for k in range(4):
        t = KT[k]
        part = nt(bt[...], wbuf[HW * t:HW * t + HW, :])
        gc_out[:, 172 * k:172 * k + 172] = part[0:216, 0:172].astype(BF16)

    wait_all(q_ag)
    for v in range(8):
        hfull[v // 4, v % 4] = nn(qt[:, 256 * v:256 * v + 256].T, actp[...])
    for v in range(2):
        hs[:, :, 64 * v:64 * v + 64, :] = hfull[:, :, rows(64 * (2 * v + far), 64), :].astype(BF16)
    h_core = push(hs, hc, core_peer)
    g.to_x(0)
    h_core.wait_recv()
    for v in range(2):
        at = slice(64 * v, 64 * v + 64)
        value = hfull[:, :, rows(64 * (2 * v + core), 64), :] + hc[:, :, at, :].astype(F32)
        ho[:, :, at, :] = value
        hh[:, :, at, :] = value.astype(BF16)
    h_y = []
    for d in (1, 2, 3):
        other = (y + d) % 4
        h_y.append(push(hh.at[other // 2, :, rows(64 * (other % 2), 64), :], hry.at[d - 1], y_peer(d)))

    g.to_z(0)
    g.to_x(1)
    g.to_z(1)

    wait_all(h_y)
    value = ho[yh, :, rows(64 * yl, 64), :]
    for d in range(3):
        value = value + hry[d].astype(F32)
    hzf[...] = value
    hzs[...] = value.astype(BF16)
    h_z = [push(hzs.at[(zhi + d) % 4], hrz.at[d - 1], z_peer(d)) for d in (1, 2, 3)]

    gs_out[0:96, :] = g.result(0).astype(BF16)
    gs_out[96:172, :] = g.result(1)[0:76, :].astype(BF16)

    wait_all(h_z)
    value = hzf[zhi]
    for d in range(3):
        value = value + hrz[d].astype(F32)
    gr_out[...] = value[:, 0:320].astype(BF16)

    for copy, cond in sent:
        if cond is None:
            copy.wait_send()
        else:
            pl.when(cond)(copy.wait_send)


def local(activations, cotangent, small_weight, grow_rows, grow_cols):
    scale = float(32 * activations.shape[0]) ** -0.5
    bf, f32 = (lambda *s: pltpu.VMEM(s, BF16)), (lambda *s: pltpu.VMEM(s, F32))

    def scatter(height):
        return [
            bf(2 * height, 2048), bf(2 * height, 2048), f32(2 * height, 2048), bf(2 * height, 2048),
            bf(3, height, 1024), f32(height, 1024), bf(height, 1024), bf(4, height, 256), bf(4, height, 256),
        ]

    scratch = [
        bf(HW, 256), bf(4 * HW, 2048), bf(2, 4, 256, LA), bf(256, 768), bf(768, 256), bf(128, LA), bf(LA, 128),
        bf(7, 128, 256), bf(7, 128, 256), bf(128, 256), bf(512, 2048),
        bf(7, FP, 256), bf(7, FP, 256), bf(FP, 2048), bf(512, 256), bf(256, 512),
        bf(7, FP, 256), bf(7, FP, 256), bf(FP, 2048),
        *scatter(HP), bf(HP, 256), bf(HP, 2048),
        *scatter(HW),
        f32(2, 4, 256, LA), bf(2, 4, 128, LA), bf(2, 4, 128, LA), f32(2, 4, 128, LA), bf(2, 4, 128, LA),
        bf(3, 4, 64, LA), f32(4, 64, LA), bf(4, 64, LA), bf(3, 64, LA),
        pltpu.SemaphoreType.DMA((NSEM,)), pltpu.SemaphoreType.DMA((NSEM,)),
    ]
    vmem = pl.BlockSpec(memory_space=pltpu.VMEM)
    gr, gc, gs = pl.pallas_call(
        functools.partial(kernel, scale),
        out_shape=(
            jax.ShapeDtypeStruct((64, 320), BF16),
            jax.ShapeDtypeStruct((216, 688), BF16),
            jax.ShapeDtypeStruct((172, 256), BF16),
        ),
        in_specs=[vmem] * 5,
        out_specs=(vmem,) * 3,
        scratch_shapes=scratch,
        compiler_params=pltpu.CompilerParams(
            collective_id=0, has_side_effects=True, vmem_limit_bytes=56 * 2**20
        ),
        cost_estimate=pl.CostEstimate(flops=3_700_000_000, bytes_accessed=3_000_000, transcendentals=110_592),
        name="grow",
    )(activations.T, cotangent.T, small_weight.T, grow_rows.T, grow_cols)
    return gr.T, gc, gs.T


def solution(mesh):
    return jax.shard_map(
        local,
        mesh=mesh,
        in_specs=(
            P("col", "row"),
            P("row", "col"),
            P("row", "col"),
            P("row", "col"),
            P("col", "row"),
        ),
        out_specs=(P("row", "col"), P("col", "row"), P("row", "col")),
        check_vma=False,
    )
```

time: 734 us -> 163 us (0.22)
  waiting for transfers between devices: 415 us -> 0 us
  blocking collectives: 250 us -> 0 us
  Pallas kernels: 0 us -> 158 us
  matrix products: 25.7 us -> 0 us
  local copies, waits for them, and re-layouts: 19.5 us -> 3.82 us
  between operations: 14.6 us -> 0.64 us
    all_gather x5 -> x0, waiting for transfers between devices: 243 us -> none  [the longest x1 65.7 us: local(): b_panel = lax.all_gather(grow_cols, 'row', axis=1, tiled=True)]
    unnamed x1 -> x0, blocking collectives: 222 us -> none
    pallas_call x0 -> x1, Pallas kernels: none -> 158 us  [local(): pl.pallas_call(functools.partial(kernel, scale), out_shape=(jax.ShapeDtyp...]
    reduce_scatter x3 -> x0, waiting for transfers between devices: 124 us -> none  [the longest x1 79.9 us: local(): lax.psum_scatter(jnp.dot(block, grown_panel, preferred_element_type=jnp.f...]
    unnamed x10 -> x0, waiting for transfers between devices: 48.1 us -> none
    all_gather x1 -> x0, blocking collectives: 28.9 us -> none  [local(): c_panel = lax.all_gather(product, 'row', axis=0, tiled=True)]
    dot_general x7 -> x0, matrix products: 25.7 us -> none  [the longest x6 19.1 us: contract(): lax.dot_general(left, right, (((left_dim,), (right_dim,)), ((), ())), pre...]
    unnamed x16 -> x5, local copies, waits for them, and re-layouts: 17.1 us -> 3.82 us
  transfers between devices with their start and end apart: 9 -> 0, of which waited for: 8 -> 0; matrix products, arithmetic and copies ran while one was open for 4% -> 0% of each run, Pallas kernels for 0% -> 0%
where the time goes in v2:
time: 163 us
  Pallas kernels  158 us (97%)
  local copies, waits for them, and re-layouts  3.82 us (2%)
    pallas_call x1, Pallas kernels, local(): pl.pallas_call(functools.partial(kernel, scale), out_shape=(jax.ShapeDtyp...  158 us
    unnamed x5, local copies, waits for them, and re-layouts  3.82 us

profile of v2, /device:TPU:33, one launch (start us, length us, event | category | flops | bytes accessed | tf_op | source)
XLA Modules:
  0.0 162.9 jit_solution(6251719895594292312)
XLA Ops:
  0.6 158.4 %grow.1 = (bf16[64,320]{1,0:T(8,128)(2,1)}, bf16[216,688]{1,0:T(8,128)(2,1)}, bf16[172,256]{1,0:T(8,128)(2,1)}) custom-call(bf16[320,128]{1,0:T(8,128)(2,1)} %bitcast.10, bf16[216,512]{1,0:T(8,128)(2,1)} %bitcast.8, bf16[172,256]{1,0:T(8,128)(2,1)} %bitcast.9, bf16[64,320]{1,0:T(8,128)(2,1)} %bitcast.11, bf16[216,688]{1,0:T(8,128)(2,1)} %b.1), custom_call_target="tpu_custom_call" | custom-call | flops 3700000000 | bytes 3000000 | tf_op jit(solution)/shard_map/grow/pallas_call | solution.py:496
  159.1 1.4 copy.11
  160.5 0.0 copy-start
  160.5 1.8 %copy.12 = bf16[216,688]{1,0:T(8,128)(2,1)} copy(bf16[216,688]{1,0:T(8,128)(2,1)} %get-tuple-element.13) | data formatting | bytes 594432
  162.2 0.0 copy-done
  162.2 0.6 copy.13
Async XLA Ops:
  160.5 1.8 %copy-start = (bf16[172,256]{1,0:T(8,128)(2,1)S(1)}, bf16[172,256]{1,0:T(8,128)(2,1)}, u32[]{:S(2)}) copy-start(bf16[172,256]{1,0:T(8,128)(2,1)} %get-tuple-element.8) | copy-start | bytes 264196

commit v3 on v0

v3 whole, which is shorter than its diff:
```python
import functools

import jax
import jax.numpy as jnp
from jax import lax
from jax.experimental import pallas as pl
from jax.experimental.pallas import tpu as pltpu
from jax.sharding import PartitionSpec as P

MESH = pl.DeviceIdType.MESH
F32 = jnp.float32
BF16 = jnp.bfloat16
HW = 176
HP = 128
FP = 224
HB = 4 * HW
LB = 768
LA = 384
NSEM = 256
KT = (0, 2, 1, 3)
CW = ((0, 96), (96, 80))


def nn(a, b):
    return jnp.dot(a, b, preferred_element_type=F32)


def nt(a, b):
    return lax.dot_general(a, b, (((1,), (1,)), ((), ())), preferred_element_type=F32)


def lanes(start, size):
    return pl.ds(pl.multiple_of(start, 128), size)


def rows(start, size):
    return pl.ds(pl.multiple_of(start, 16), size)


def kernel(
    scale,
    act_in, cot_in, w_in, a_in, b_in,
    gr_out, gc_out, gs_out,
    act, cot, w, a, b, gc,
    wpad, wbuf, bbuf, bbuft, apad, abuf, axb,
    pbuf, ct, delta, dt,
    bs, brcv, bt,
    qfar, qgot, qown, qhalf, qry, qyf, qys, qrz, qt,
    gfar, ggot, gown, ghalf, gry, gyf, gys, grz,
    gcs, gcx, gcf, gcn, gcz,
    hfull, hs, hc, hh, hy, hyf, hys, hr,
    ssem, rsem, lsem,
):
    r = lax.axis_index("row")
    c = lax.axis_index("col")
    x, zlo = r // 2, r % 2
    zhi, y, core = c // 8, (c // 2) % 4, c % 2
    yh, yl = y // 2, y % 2
    kt = 2 * core + yl
    kn = 2 * yl + core
    far = 1 - core
    near_row = r + 1 - 2 * zlo
    stays = jnp.logical_and(x == zhi, zlo == yh)

    def row_peer(d):
        return ((r + d) % 8, c)

    def y_peer(d):
        return (r, zhi * 8 + ((y + d) % 4) * 2 + core)

    def z_peer(d):
        return (r, ((zhi + d) % 4) * 8 + y * 2 + core)

    core_peer = (r, c + 1 - 2 * core)
    pair_peer = (r, zhi * 8 + (y + 1 - 2 * yl) * 2 + core)

    def swap_target(j):
        return (zhi * 2 + yh, j * 8 + zlo * 4 + yl * 2 + core)

    def swap_source(s):
        return (s * 2 + yh, x * 8 + zlo * 4 + yl * 2 + core)

    used = [0]
    sent = []

    def push(src, dst, device):
        i = used[0]
        used[0] += 1
        copy = pltpu.make_async_remote_copy(
            src_ref=src, dst_ref=dst, send_sem=ssem.at[i], recv_sem=rsem.at[i],
            device_id=device, device_id_type=MESH,
        )
        copy.start()
        sent.append((copy, None))
        return copy

    def wait_all(copies):
        for copy in copies:
            copy.wait_recv()

    barrier = pltpu.get_barrier_semaphore()

    def greet(device):
        pl.semaphore_signal(barrier, inc=1, device_id=device, device_id_type=MESH)

    for d in range(1, 8):
        greet(row_peer(d))
    for d in range(1, 4):
        greet(y_peer(d))
        greet(z_peer(d))
    greet(core_peer)
    for s in range(4):
        pl.when(jnp.logical_not(jnp.logical_and(stays, x == s)))(lambda s=s: greet(swap_source(s)))

    loads = [
        pltpu.make_async_copy(src, dst, lsem.at[i])
        for i, (src, dst) in enumerate(((act_in, act), (w_in, w), (a_in, a), (b_in, b), (cot_in, cot)))
    ]
    for load in loads:
        load.start()
    bbuf[:, FP:256, :] = jnp.zeros((8, 256 - FP, LB), BF16)
    bbuf[r] = jnp.zeros((256, LB), BF16)
    loads[1].wait()
    wpad[0:172, :] = w[...]
    wpad[172:HW, :] = jnp.zeros((HW - 172, 256), BF16)
    wbuf[zhi, rows(HW * (2 * y + core), HW), :] = wpad[...]
    loads[2].wait()
    apad[:, 0:320] = a[...]
    apad[:, 320:LA] = jnp.zeros((64, LA - 320), BF16)
    arow = rows(64 * kn, 64)
    abuf[arow, lanes(LA * r, LA)] = apad[...]
    loads[3].wait()
    for k in range(4):
        bbuf[r, 0:216, HW * k:HW * k + 172] = b[:, 172 * k:172 * k + 172]
    loads[0].wait()

    @pl.when(stays)
    def _():
        pl.semaphore_wait(barrier, 17)

    @pl.when(jnp.logical_not(stays))
    def _():
        pl.semaphore_wait(barrier, 18)

    class RowGather:
        def __init__(self, at):
            self.at = at

        def start(self):
            block = self.at(r)
            self.copies = [push(block, block, row_peer(2 * d)) for d in (1, 2, 3)]
            self.near = push(block, block, (near_row, c))

        def forward(self):
            self.near.wait_recv()
            block = self.at(near_row)
            self.copies += [push(block, block, row_peer(2 * d)) for d in (1, 2, 3)]

        def finish(self):
            wait_all(self.copies)

    class ColGather:
        def __init__(self, at, band):
            self.at, self.band = at, band
            self.y, self.core = [], []

        def start(self):
            block = self.at(zhi)
            self.z = [push(block, block, z_peer(d)) for d in (1, 2, 3)]

        def along_y(self, e):
            if e:
                self.z[e - 1].wait_recv()
            block = self.at((zhi + 4 - e) % 4)
            self.y.append([push(block, block, y_peer(d)) for d in (1, 2, 3)])

        def to_core(self, d):
            if d:
                for e in range(4):
                    self.y[e][d - 1].wait_recv()
            block = self.band((y + 4 - d) % 4)
            self.core.append(push(block, block, core_peer))

        def finish(self):
            wait_all(self.core)

    gather_w = ColGather(
        lambda z: wbuf.at[z, rows(HW * (2 * y + core), HW), :],
        lambda other: wbuf.at[:, rows(HW * (2 * other + core), HW), :])
    gather_a = RowGather(lambda row: abuf.at[arow, lanes(LA * row, LA)])
    gather_b = RowGather(lambda row: bbuf.at[row, 0:FP, :])

    base = used[0]
    used[0] += 4
    for d in range(4):
        copy = pltpu.make_async_remote_copy(
            src_ref=act, dst_ref=axb.at[zlo, x], send_sem=ssem.at[base + d], recv_sem=rsem.at[base + x],
            device_id=swap_target((zhi + d) % 4), device_id_type=MESH,
        )
        if d:
            copy.start()
            sent.append((copy, None))
        else:
            pl.when(jnp.logical_not(stays))(copy.start)
            sent.append((copy, jnp.logical_not(stays)))

    @pl.when(stays)
    def _():
        axb[zlo, x] = act[...]

    def act_wait():
        for s in range(4):
            copy = pltpu.make_async_remote_copy(
                src_ref=act, dst_ref=axb.at[zlo, x], send_sem=ssem.at[base], recv_sem=rsem.at[base + s],
                device_id=core_peer, device_id_type=MESH,
            )
            pl.when(jnp.logical_not(jnp.logical_and(stays, x == s)))(copy.wait_recv)

    gather_a.start()
    gather_w.start()
    gather_w.along_y(0)
    gather_b.start()
    gather_a.forward()
    gather_w.along_y(1)
    gather_w.along_y(2)
    gather_w.along_y(3)
    gather_a.finish()
    a_rows = abuf.at[arow, :]
    a_pair = push(a_rows, a_rows, pair_peer)
    a_core = [push(a_rows, a_rows, core_peer)]
    act_wait()
    act_y = push(axb.at[yh], axb.at[yh], y_peer(2))
    gather_b.forward()
    gather_w.to_core(0)
    a_pair.wait_recv()
    a_rows = abuf.at[rows(64 * (2 * (1 - yl) + core), 64), :]
    a_core.append(push(a_rows, a_rows, core_peer))
    dt[...] = jnp.zeros_like(dt)
    bt[...] = jnp.zeros_like(bt)
    wait_all(a_core)
    act_y.wait_recv()

    total = nn(abuf[:, 0:320], axb[0, 0])
    for v in range(1, 8):
        total = total + nn(abuf[:, LA * v:LA * v + 320], axb[v % 2, v // 2])
    prow = rows(HP * kt, HP)
    pbuf[prow, lanes(1024 * yh + 256 * zhi, 256)] = total.T.astype(BF16)
    gather_p = ColGather(
        lambda z: pbuf.at[prow, lanes(1024 * yh + 256 * z, 256)],
        lambda other: pbuf.at[rows(HP * (2 * core + other % 2), HP), lanes(1024 * (other // 2), 1024)])
    gather_p.start()
    gather_p.along_y(0)
    for d in (1, 2, 3):
        gather_w.to_core(d)
    for e in (1, 2, 3):
        gather_p.along_y(e)
    gather_p.to_core(0)
    gather_w.finish()

    def chain_term(row):
        return nn(bbuf[row, 0:FP, 0:HB], wbuf[row // 2, rows(HB * (row % 2), HB), :])

    total = chain_term(r) + chain_term(near_row)
    gather_b.finish()
    for d in (1, 2, 3):
        total = total + chain_term((r + 2 * d) % 8) + chain_term((near_row + 2 * d) % 8)

    def panel(row):
        return lanes(1024 * (row % 2) + 256 * (row // 2), 256)

    own = panel(r)
    ct[:, own] = total.astype(BF16)
    gather_c = RowGather(lambda row: ct.at[:, panel(row)])
    gather_c.start()
    gather_c.forward()
    for v in range(8):
        bbuft[v] = bbuf[v].T
    for d in (1, 2, 3):
        gather_p.to_core(d)
    gather_p.finish()
    loads[4].wait()
    gather_c.finish()

    for k in range(4):
        t = KT[k]
        hidden = nt(ct[...], pbuf[HP * t:HP * t + HP, :])[0:216, :]
        s = 1.0 / (1.0 + jnp.exp(-hidden))
        grad = cot[:, HP * k:HP * k + HP].astype(F32) * s * (1.0 + hidden * (1.0 - s))
        dt[0:216, HP * t:HP * t + HP] = grad.astype(BF16)

    b_rs = []
    for d in range(1, 8):
        bs[d - 1] = nn(dt[0:FP, :], pbuf[:, panel((r + d) % 8)]).astype(BF16)
        b_rs.append(push(bs.at[d - 1], brcv.at[d - 1], row_peer(d)))
    delta[...] = dt[...].T

    def tiles(body):
        lax.fori_loop(0, 8, lambda i, _: (body(lanes(256 * i, 256)), 0)[1], 0)

    def q_far(at):
        qfar[:, at] = nn(delta[rows(2 * HP * far, 2 * HP), 0:FP], ct[:, at]).astype(BF16)

    def q_own(at):
        qown[:, at] = nn(delta[rows(2 * HP * core, 2 * HP), 0:FP], ct[:, at])

    def q_sum(at):
        value = qown[:, at] + qgot[:, at].astype(F32)
        qown[:, at] = value
        qhalf[:, at] = value.astype(BF16)

    tiles(q_far)
    q_core = push(qfar, qgot, core_peer)
    tiles(q_own)
    back = nn(dt[0:FP, :], pbuf[:, own])
    q_core.wait_recv()
    tiles(q_sum)
    q_y = []
    for d in (1, 2, 3):
        other = (y + d) % 4
        q_y.append(push(
            qhalf.at[rows(HP * (other % 2), HP), lanes(1024 * (other // 2), 1024)], qry.at[d - 1], y_peer(d)))

    for d in range(7):
        b_rs[d].wait_recv()
        back = back + brcv[d].astype(F32)
    bt[0:FP, :] = (back * scale).astype(BF16)

    def cols_term(row):
        return nt(bt[0:FP, :], wbuf[row // 2, rows(HB * (row % 2), HB), :])

    gc_x = []
    for i, base_row in enumerate((near_row, r)):
        for d in (1, 2, 3):
            slot = 3 * i + d - 1
            gcs[slot, :, 0:HB] = cols_term((base_row + 2 * d) % 8).astype(BF16)
            gc_x.append(push(gcs.at[slot], gcx.at[slot], row_peer(2 * d)))

    def small_term(v, u, which):
        return nn(bbuft[v, rows(HW * (2 * u + which), HW), :], bt[...])

    for v in range(8):
        for u in range(2):
            gfar[v // 2, 2 * (v % 2) + u] = small_term(v, u, far).astype(BF16)
    g_core = push(gfar, ggot, core_peer)
    for v in range(8):
        for u in range(2):
            gown[v // 2, 2 * (v % 2) + u] = small_term(v, u, core)
    gcn[...] = cols_term(near_row)
    gcf[...] = cols_term(r)
    g_core.wait_recv()

    def g_sum(i, _):
        value = gown[i // 4, i % 4] + ggot[i // 4, i % 4].astype(F32)
        gown[i // 4, i % 4] = value
        ghalf[i // 4, i % 4] = value.astype(BF16)
        return 0

    lax.fori_loop(0, 16, g_sum, 0)
    g_y = [
        [push(ghalf.at[:, (y + d) % 4, off:off + size, :], gry.at[d - 1, :, off:off + size, :], y_peer(d))
         for d in (1, 2, 3)]
        for off, size in CW
    ]

    wait_all(q_y)
    for v in range(4):
        at = slice(256 * v, 256 * v + 256)
        value = qown[rows(HP * yl, HP), lanes(1024 * yh + 256 * v, 256)]
        for d in range(3):
            value = value + qry[d, :, at].astype(F32)
        qyf[:, at] = value
        qys[:, at] = value.astype(BF16)
    q_z = [push(qys.at[:, lanes(256 * ((zhi + d) % 4), 256)], qrz.at[d - 1], z_peer(d)) for d in (1, 2, 3)]

    wait_all(gc_x[0:3])
    value = gcn[...]
    for d in range(3):
        value = value + gcx[d, :, 0:HB].astype(F32)
    gcs[6, :, 0:HB] = value.astype(BF16)
    gc_z = push(gcs.at[6], gcz, (near_row, c))

    wait_all(q_z)
    value = qyf[:, lanes(256 * zhi, 256)]
    for d in range(3):
        value = value + qrz[d].astype(F32)
    qt[...] = (value * scale).T.astype(BF16)
    for v in range(8):
        hfull[v, :, 0:320] = nt(qt[...], axb[v % 2, v // 2])
    for u in range(2):
        hs[:, 64 * u:64 * u + 64, 0:320] = hfull[:, rows(64 * (2 * u + far), 64), 0:320].astype(BF16)
    h_core = push(hs, hc, core_peer)

    def small_z(i):
        off, size = CW[i]
        wait_all(g_y[i])
        for v in range(4):
            value = gown[v, y, off:off + size, :]
            for d in range(3):
                value = value + gry[d, v, off:off + size, :].astype(F32)
            gyf[v, off:off + size, :] = value
            gys[v, off:off + size, :] = value.astype(BF16)
        return [
            push(gys.at[(zhi + d) % 4, off:off + size, :], grz.at[d - 1, off:off + size, :], z_peer(d))
            for d in (1, 2, 3)
        ]

    h_core.wait_recv()
    for v in range(8):
        for u in range(2):
            at = slice(64 * u, 64 * u + 64)
            value = hfull[v, rows(64 * (2 * u + core), 64), 0:320] + hc[v, at, 0:320].astype(F32)
            hfull[v, rows(64 * (2 * u + core), 64), 0:320] = value
            hh[u, v, :, 0:320] = value.astype(BF16)
    h_pair = push(hh.at[1 - yl], hy, pair_peer)

    g_z = [small_z(0)]

    h_pair.wait_recv()
    for v in range(8):
        value = hfull[v, rows(64 * kn, 64), 0:320] + hy[v, :, 0:320].astype(F32)
        hyf[v, :, 0:320] = value
        hys[v, :, 0:320] = value.astype(BF16)
    h_r = [push(hys.at[(r + d) % 8], hr.at[d - 1], row_peer(d)) for d in range(1, 8)]

    g_z.append(small_z(1))

    wait_all(gc_x[3:6])
    value = gcf[...]
    for d in range(3):
        value = value + gcx[3 + d, :, 0:HB].astype(F32)
    gc_z.wait_recv()
    value = (value + gcz[:, 0:HB].astype(F32)).astype(BF16)
    for k in range(4):
        gc[:, 172 * k:172 * k + 172] = value[0:216, HW * k:HW * k + 172]
    gc_copy = pltpu.make_async_copy(gc, gc_out, lsem.at[5])
    gc_copy.start()

    wait_all(h_r)
    value = hyf[r, :, 0:320]
    for d in range(7):
        value = value + hr[d, :, 0:320].astype(F32)
    gr_out[...] = value.astype(BF16)

    for copies in g_z:
        wait_all(copies)
    value = gyf[zhi]
    for d in range(3):
        value = value + grz[d].astype(F32)
    gs_out[...] = value[0:172, :].astype(BF16)

    gc_copy.wait()
    for copy, cond in sent:
        if cond is None:
            copy.wait_send()
        else:
            pl.when(cond)(copy.wait_send)


def local(activations, cotangent, small_weight, grow_rows, grow_cols):
    scale = float(32 * activations.shape[0]) ** -0.5
    bf, f32 = (lambda *s: pltpu.VMEM(s, BF16)), (lambda *s: pltpu.VMEM(s, F32))
    scratch = [
        bf(320, 128), bf(216, 512), bf(172, 256), bf(64, 320), bf(216, 688), bf(216, 688),
        bf(HW, 256), bf(4, 8 * HW, 256), bf(8, 256, LB), bf(8, LB, 256), bf(64, LA), bf(256, 8 * LA),
        bf(2, 4, 320, 128),
        bf(512, 2048), bf(FP, 2048), bf(512, 256), bf(256, 512),
        bf(7, FP, 256), bf(7, FP, 256), bf(256, 256),
        bf(2 * HP, 2048), bf(2 * HP, 2048), f32(2 * HP, 2048), bf(2 * HP, 2048),
        bf(3, HP, 1024), f32(HP, 1024), bf(HP, 1024), bf(3, HP, 256), bf(256, 128),
        bf(4, 4, HW, 256), bf(4, 4, HW, 256), f32(4, 4, HW, 256), bf(4, 4, HW, 256),
        bf(3, 4, HW, 256), f32(4, HW, 256), bf(4, HW, 256), bf(3, HW, 256),
        bf(7, FP, LB), bf(6, FP, LB), f32(FP, HB), f32(FP, HB), bf(FP, LB),
        f32(8, 256, LA), bf(8, 128, LA), bf(8, 128, LA), bf(2, 8, 64, LA), bf(8, 64, LA),
        f32(8, 64, LA), bf(8, 64, LA), bf(7, 64, LA),
        pltpu.SemaphoreType.DMA((NSEM,)), pltpu.SemaphoreType.DMA((NSEM,)), pltpu.SemaphoreType.DMA((6,)),
    ]
    vmem, hbm = pl.BlockSpec(memory_space=pltpu.VMEM), pl.BlockSpec(memory_space=pl.ANY)
    gr, gc, gs = pl.pallas_call(
        functools.partial(kernel, scale),
        out_shape=(
            jax.ShapeDtypeStruct((64, 320), BF16),
            jax.ShapeDtypeStruct((216, 688), BF16),
            jax.ShapeDtypeStruct((172, 256), BF16),
        ),
        in_specs=[hbm] * 5,
        out_specs=(vmem, hbm, vmem),
        scratch_shapes=scratch,
        compiler_params=pltpu.CompilerParams(
            collective_id=0, has_side_effects=True, vmem_limit_bytes=60 * 2**20
        ),
        cost_estimate=pl.CostEstimate(flops=3_700_000_000, bytes_accessed=3_000_000, transcendentals=110_592),
        name="grow",
    )(activations.T, cotangent.T, small_weight.T, grow_rows.T, grow_cols)
    return gr.T, gc, gs.T


def solution(mesh):
    return jax.shard_map(
        local,
        mesh=mesh,
        in_specs=(
            P("col", "row"),
            P("row", "col"),
            P("row", "col"),
            P("row", "col"),
            P("col", "row"),
        ),
        out_specs=(P("row", "col"), P("col", "row"), P("row", "col")),
        check_vma=False,
    )
```

time: 734 us -> 145 us (0.20)
  waiting for transfers between devices: 415 us -> 0 us
  blocking collectives: 250 us -> 0 us
  Pallas kernels: 0 us -> 138 us
  matrix products: 25.7 us -> 0 us
  local copies, waits for them, and re-layouts: 19.5 us -> 3.82 us
  between operations: 14.6 us -> 0.64 us
    all_gather x5 -> x0, waiting for transfers between devices: 243 us -> none  [the longest x1 65.7 us: local(): b_panel = lax.all_gather(grow_cols, 'row', axis=1, tiled=True)]
    unnamed x1 -> x0, blocking collectives: 222 us -> none
    pallas_call x0 -> x1, Pallas kernels: none -> 138 us  [local(): pl.pallas_call(functools.partial(kernel, scale), out_shape=(jax.ShapeDtyp...]
    reduce_scatter x3 -> x0, waiting for transfers between devices: 124 us -> none  [the longest x1 79.9 us: local(): lax.psum_scatter(jnp.dot(block, grown_panel, preferred_element_type=jnp.f...]
    unnamed x10 -> x0, waiting for transfers between devices: 48.1 us -> none
    all_gather x1 -> x0, blocking collectives: 28.9 us -> none  [local(): c_panel = lax.all_gather(product, 'row', axis=0, tiled=True)]
    dot_general x7 -> x0, matrix products: 25.7 us -> none  [the longest x6 19.1 us: contract(): lax.dot_general(left, right, (((left_dim,), (right_dim,)), ((), ())), pre...]
    unnamed x16 -> x5, local copies, waits for them, and re-layouts: 17.1 us -> 3.82 us
  transfers between devices with their start and end apart: 9 -> 0, of which waited for: 8 -> 0; matrix products, arithmetic and copies ran while one was open for 4% -> 0% of each run, Pallas kernels for 0% -> 0%
where the time goes in v3:
time: 145 us; the launch traced here: 142 us
  Pallas kernels  138 us (95%)
  local copies, waits for them, and re-layouts  3.82 us (3%)
    pallas_call x1, Pallas kernels, local(): pl.pallas_call(functools.partial(kernel, scale), out_shape=(jax.ShapeDtyp...  138 us
    unnamed x5, local copies, waits for them, and re-layouts  3.82 us

profile of v3, /device:TPU:33, one launch (start us, length us, event | category | flops | bytes accessed | tf_op | source)
XLA Modules:
  0.0 142.1 jit_solution(12834344952313443463)
XLA Ops:
  0.6 137.6 %grow.1 = (bf16[64,320]{1,0:T(8,128)(2,1)}, bf16[216,688]{1,0:T(8,128)(2,1)}, bf16[172,256]{1,0:T(8,128)(2,1)}) custom-call(bf16[320,128]{1,0:T(8,128)(2,1)} %bitcast.10, bf16[216,512]{1,0:T(8,128)(2,1)} %bitcast.8, bf16[172,256]{1,0:T(8,128)(2,1)} %bitcast.9, bf16[64,320]{1,0:T(8,128)(2,1)} %bitcast.11, bf16[216,688]{1,0:T(8,128)(2,1)} %b_in.1), custom_call_target="tpu_custom_call" | custom-call | flops 3700000000 | bytes 3000000 | tf_op jit(solution)/shard_map/grow/pallas_call | solution.py:478
  138.3 1.4 %copy.11 = bf16[320,64]{0,1:T(8,128)(2,1)} copy(bf16[320,64]{0,1:T(8,128)(2,1)} %bitcast.7) | data formatting | bytes 81920
  139.7 0.0 copy-start
  139.7 1.8 %copy.12 = bf16[216,688]{1,0:T(8,128)(2,1)} copy(bf16[216,688]{1,0:T(8,128)(2,1)} %get-tuple-element.13) | data formatting | bytes 594432
  141.4 0.0 copy-done
  141.4 0.6 copy.13
Async XLA Ops:
  139.7 1.8 %copy-start = (bf16[172,256]{1,0:T(8,128)(2,1)S(1)}, bf16[172,256]{1,0:T(8,128)(2,1)}, u32[]{:S(2)}) copy-start(bf16[172,256]{1,0:T(8,128)(2,1)} %get-tuple-element.8) | copy-start | bytes 264196

commit v4 on v3

--- a/solution.py
+++ b/solution.py
@@ -19,6 +19,7 @@
 NSEM = 256
 KT = (0, 2, 1, 3)
 CW = ((0, 96), (96, 80))
+CQ = ((0, 64), (64, 64))
 
 
 def nn(a, b):
@@ -47,8 +48,8 @@
     bs, brcv, bt,
     qfar, qgot, qown, qhalf, qry, qyf, qys, qrz, qt,
     gfar, ggot, gown, ghalf, gry, gyf, gys, grz,
-    gcs, gcx, gcf, gcn, gcz,
-    hfull, hs, hc, hh, hy, hyf, hys, hr,
+    gcs, gcx, gcr, gce, gcf, gcn, gcz,
+    hfull, hs, hc, hh, hyf, hr, hp, hq, hy,
     ssem, rsem, lsem,
 ):
     r = lax.axis_index("row")
@@ -127,8 +128,10 @@
     loads[2].wait()
     apad[:, 0:320] = a[...]
     apad[:, 320:LA] = jnp.zeros((64, LA - 320), BF16)
-    arow = rows(64 * kn, 64)
+    arow = rows(64 * kt, 64)
+    acore = rows(128 * core, 128)
     abuf[arow, lanes(LA * r, LA)] = apad[...]
+
     loads[3].wait()
     for k in range(4):
         bbuf[r, 0:216, HW * k:HW * k + 172] = b[:, 172 * k:172 * k + 172]
@@ -149,6 +152,9 @@
         def start(self):
             block = self.at(r)
             self.copies = [push(block, block, row_peer(2 * d)) for d in (1, 2, 3)]
+
+        def start_near(self):
+            block = self.at(r)
             self.near = push(block, block, (near_row, c))
 
         def forward(self):
@@ -158,6 +164,26 @@
 
         def finish(self):
             wait_all(self.copies)
+
+    class RingGather:
+        def __init__(self, row, whole, half):
+            self.row, self.whole, self.half = row, whole, half
+
+        def start(self):
+            block = self.whole(self.row)
+            self.ahead = push(block, block, row_peer(2))
+            self.behind = push(block, block, row_peer(6))
+
+        def relay(self):
+            self.ahead.wait_recv()
+            block = self.half((self.row + 6) % 8, 0)
+            self.rest = [push(block, block, row_peer(2))]
+            self.behind.wait_recv()
+            block = self.half((self.row + 2) % 8, 1)
+            self.rest.append(push(block, block, row_peer(6)))
+
+        def finish(self):
+            wait_all(self.rest)
 
     class ColGather:
         def __init__(self, at, band):
@@ -187,8 +213,13 @@
     gather_w = ColGather(
         lambda z: wbuf.at[z, rows(HW * (2 * y + core), HW), :],
         lambda other: wbuf.at[:, rows(HW * (2 * other + core), HW), :])
-    gather_a = RowGather(lambda row: abuf.at[arow, lanes(LA * row, LA)])
-    gather_b = RowGather(lambda row: bbuf.at[row, 0:FP, :])
+    gather_a = RowGather(lambda row: abuf.at[acore, lanes(LA * row, LA)])
+    b_parts = (lambda row: bbuf.at[row, 0:FP, :]), (lambda row, i: bbuf.at[row, 112 * i:112 * i + 112, :])
+    gather_b = RingGather(r, *b_parts)
+    gather_bn = RingGather(near_row, *b_parts)
+    b_near = push(bbuf.at[r, 0:FP, :], bbuf.at[r, 0:FP, :], (near_row, c))
+    gather_b.start()
+
 
     base = used[0]
     used[0] += 4
@@ -216,62 +247,64 @@
             )
             pl.when(jnp.logical_not(jnp.logical_and(stays, x == s)))(copy.wait_recv)
 
+    a_block = abuf.at[arow, lanes(LA * r, LA)]
+    a_pair = push(a_block, a_block, pair_peer)
+    gather_w.along_y(0)
+    gather_b.relay()
+    a_pair.wait_recv()
+    gather_a.start_near()
     gather_a.start()
-    gather_w.start()
-    gather_w.along_y(0)
-    gather_b.start()
-    gather_a.forward()
-    gather_w.along_y(1)
-    gather_w.along_y(2)
-    gather_w.along_y(3)
-    gather_a.finish()
-    a_rows = abuf.at[arow, :]
-    a_pair = push(a_rows, a_rows, pair_peer)
-    a_core = [push(a_rows, a_rows, core_peer)]
+    b_near.wait_recv()
+    gather_bn.start()
+    dt[...] = jnp.zeros_like(dt)
+    bt[...] = jnp.zeros_like(bt)
     act_wait()
     act_y = push(axb.at[yh], axb.at[yh], y_peer(2))
-    gather_b.forward()
-    gather_w.to_core(0)
-    a_pair.wait_recv()
-    a_rows = abuf.at[rows(64 * (2 * (1 - yl) + core), 64), :]
-    a_core.append(push(a_rows, a_rows, core_peer))
-    dt[...] = jnp.zeros_like(dt)
-    bt[...] = jnp.zeros_like(bt)
-    wait_all(a_core)
+    gather_w.start()
+    gather_a.forward()
+    gather_bn.relay()
+    for e in (1, 2, 3):
+        gather_w.along_y(e)
+    gather_a.finish()
+    a_core = push(abuf.at[acore, :], abuf.at[acore, :], core_peer)
+
+    a_core.wait_recv()
     act_y.wait_recv()
-
     total = nn(abuf[:, 0:320], axb[0, 0])
     for v in range(1, 8):
         total = total + nn(abuf[:, LA * v:LA * v + 320], axb[v % 2, v // 2])
     prow = rows(HP * kt, HP)
-    pbuf[prow, lanes(1024 * yh + 256 * zhi, 256)] = total.T.astype(BF16)
+    pbuf[prow, lanes(1024 * yh + 256 * zhi, 256)] = jnp.concatenate(
+        [total[0:64], total[128:192], total[64:128], total[192:256]], axis=0).T.astype(BF16)
     gather_p = ColGather(
         lambda z: pbuf.at[prow, lanes(1024 * yh + 256 * z, 256)],
         lambda other: pbuf.at[rows(HP * (2 * core + other % 2), HP), lanes(1024 * (other // 2), 1024)])
     gather_p.start()
     gather_p.along_y(0)
-    for d in (1, 2, 3):
+    for d in range(4):
         gather_w.to_core(d)
     for e in (1, 2, 3):
         gather_p.along_y(e)
     gather_p.to_core(0)
-    gather_w.finish()
 
     def chain_term(row):
         return nn(bbuf[row, 0:FP, 0:HB], wbuf[row // 2, rows(HB * (row % 2), HB), :])
 
+    def panel(row):
+        return lanes(1024 * (row % 2) + 256 * (row // 2), 256)
+
+    own = panel(r)
+    gather_w.finish()
     total = chain_term(r) + chain_term(near_row)
     gather_b.finish()
+    gather_bn.finish()
     for d in (1, 2, 3):
         total = total + chain_term((r + 2 * d) % 8) + chain_term((near_row + 2 * d) % 8)
-
-    def panel(row):
-        return lanes(1024 * (row % 2) + 256 * (row // 2), 256)
-
-    own = panel(r)
     ct[:, own] = total.astype(BF16)
     gather_c = RowGather(lambda row: ct.at[:, panel(row)])
+    gather_c.start_near()
     gather_c.start()
+
     gather_c.forward()
     for v in range(8):
         bbuft[v] = bbuf[v].T
@@ -288,37 +321,35 @@
         grad = cot[:, HP * k:HP * k + HP].astype(F32) * s * (1.0 + hidden * (1.0 - s))
         dt[0:216, HP * t:HP * t + HP] = grad.astype(BF16)
 
+    delta[...] = dt[...].T
+
+    def tiles(body):
+        lax.fori_loop(0, 8, lambda i, _: (body(lanes(256 * i, 256)), 0)[1], 0)
+
+    def q_far(at):
+        qfar[:, at] = nn(delta[rows(2 * HP * far, 2 * HP), 0:FP], ct[:, at]).astype(BF16)
+
+    def q_sum(at):
+        value = nn(delta[rows(2 * HP * core, 2 * HP), 0:FP], ct[:, at]) + qgot[:, at].astype(F32)
+        qown[:, at] = value
+        qhalf[:, at] = value.astype(BF16)
+
+    tiles(q_far)
+    q_core = push(qfar, qgot, core_peer)
+
     b_rs = []
     for d in range(1, 8):
         bs[d - 1] = nn(dt[0:FP, :], pbuf[:, panel((r + d) % 8)]).astype(BF16)
         b_rs.append(push(bs.at[d - 1], brcv.at[d - 1], row_peer(d)))
-    delta[...] = dt[...].T
-
-    def tiles(body):
-        lax.fori_loop(0, 8, lambda i, _: (body(lanes(256 * i, 256)), 0)[1], 0)
-
-    def q_far(at):
-        qfar[:, at] = nn(delta[rows(2 * HP * far, 2 * HP), 0:FP], ct[:, at]).astype(BF16)
-
-    def q_own(at):
-        qown[:, at] = nn(delta[rows(2 * HP * core, 2 * HP), 0:FP], ct[:, at])
-
-    def q_sum(at):
-        value = qown[:, at] + qgot[:, at].astype(F32)
-        qown[:, at] = value
-        qhalf[:, at] = value.astype(BF16)
-
-    tiles(q_far)
-    q_core = push(qfar, qgot, core_peer)
-    tiles(q_own)
     back = nn(dt[0:FP, :], pbuf[:, own])
+
     q_core.wait_recv()
     tiles(q_sum)
-    q_y = []
-    for d in (1, 2, 3):
-        other = (y + d) % 4
-        q_y.append(push(
-            qhalf.at[rows(HP * (other % 2), HP), lanes(1024 * (other // 2), 1024)], qry.at[d - 1], y_peer(d)))
+    q_y = [
+        [push(qhalf.at[rows(HP * ((y + d) % 2) + off, size), lanes(1024 * (((y + d) % 4) // 2), 1024)],
+              qry.at[d - 1, off:off + size, :], y_peer(d)) for d in (1, 2, 3)]
+        for off, size in CQ
+    ]
 
     for d in range(7):
         b_rs[d].wait_recv()
@@ -328,12 +359,38 @@
     def cols_term(row):
         return nt(bt[0:FP, :], wbuf[row // 2, rows(HB * (row % 2), HB), :])
 
-    gc_x = []
-    for i, base_row in enumerate((near_row, r)):
-        for d in (1, 2, 3):
-            slot = 3 * i + d - 1
-            gcs[slot, :, 0:HB] = cols_term((base_row + 2 * d) % 8).astype(BF16)
-            gc_x.append(push(gcs.at[slot], gcx.at[slot], row_peer(2 * d)))
+    class RingSum:
+        def __init__(self, i, row):
+            self.i, self.row = i, row
+
+        def start(self):
+            self.relayed = []
+            for d, slot in ((2, 0), (1, 1), (3, 2)):
+                gcs[self.i, slot, :, 0:HB] = cols_term((self.row + 2 * d) % 8).astype(BF16)
+                if d == 2:
+                    for h, peer in ((0, 2), (1, 6)):
+                        self.relayed.append(push(
+                            gcs.at[self.i, 0, 112 * h:112 * h + 112, :], gcr.at[self.i, h], row_peer(peer)))
+            self.direct = []
+            for slot, h, peer in ((1, 1, 2), (2, 0, 6)):
+                block = slice(112 * h, 112 * h + 112)
+                self.direct.append(push(
+                    gcs.at[self.i, slot, block, :], gcx.at[self.i, slot - 1, block, :], row_peer(peer)))
+
+        def relay(self):
+            for slot, h, peer in ((1, 0, 2), (2, 1, 6)):
+                block = slice(112 * h, 112 * h + 112)
+                self.relayed[h].wait_recv()
+                value = gcs[self.i, slot, block, 0:HB].astype(F32) + gcr[self.i, h, :, 0:HB].astype(F32)
+                gcs[self.i, slot, block, 0:HB] = value.astype(BF16)
+                self.direct.append(push(
+                    gcs.at[self.i, slot, block, :], gcx.at[self.i, slot - 1, block, :], row_peer(peer)))
+
+        def result(self, value):
+            wait_all(self.direct)
+            return value + gcx[self.i, 0, :, 0:HB].astype(F32) + gcx[self.i, 1, :, 0:HB].astype(F32)
+
+    cols_near, cols_own = RingSum(0, near_row), RingSum(1, r)
 
     def small_term(v, u, which):
         return nn(bbuft[v, rows(HW * (2 * u + which), HW), :], bt[...])
@@ -342,44 +399,43 @@
         for u in range(2):
             gfar[v // 2, 2 * (v % 2) + u] = small_term(v, u, far).astype(BF16)
     g_core = push(gfar, ggot, core_peer)
+
+    q_z = []
+    for i, (off, size) in enumerate(CQ):
+        wait_all(q_y[i])
+        part = slice(off, off + size)
+        for v in range(4):
+            at = slice(256 * v, 256 * v + 256)
+            value = qown[rows(HP * yl + off, size), lanes(1024 * yh + 256 * v, 256)]
+            for d in range(3):
+                value = value + qry[d, part, at].astype(F32)
+            qyf[part, at] = value
+            qys[part, at] = value.astype(BF16)
+        q_z.append([
+            push(qys.at[part, lanes(256 * ((zhi + d) % 4), 256)], qrz.at[d - 1, part, :], z_peer(d))
+            for d in (1, 2, 3)
+        ])
+
+    cols_near.start()
+    g_core.wait_recv()
     for v in range(8):
         for u in range(2):
-            gown[v // 2, 2 * (v % 2) + u] = small_term(v, u, core)
-    gcn[...] = cols_term(near_row)
-    gcf[...] = cols_term(r)
-    g_core.wait_recv()
-
-    def g_sum(i, _):
-        value = gown[i // 4, i % 4] + ggot[i // 4, i % 4].astype(F32)
-        gown[i // 4, i % 4] = value
-        ghalf[i // 4, i % 4] = value.astype(BF16)
-        return 0
-
-    lax.fori_loop(0, 16, g_sum, 0)
-    g_y = [
-        [push(ghalf.at[:, (y + d) % 4, off:off + size, :], gry.at[d - 1, :, off:off + size, :], y_peer(d))
-         for d in (1, 2, 3)]
-        for off, size in CW
-    ]
-
-    wait_all(q_y)
-    for v in range(4):
-        at = slice(256 * v, 256 * v + 256)
-        value = qown[rows(HP * yl, HP), lanes(1024 * yh + 256 * v, 256)]
-        for d in range(3):
-            value = value + qry[d, :, at].astype(F32)
-        qyf[:, at] = value
-        qys[:, at] = value.astype(BF16)
-    q_z = [push(qys.at[:, lanes(256 * ((zhi + d) % 4), 256)], qrz.at[d - 1], z_peer(d)) for d in (1, 2, 3)]
-
-    wait_all(gc_x[0:3])
-    value = gcn[...]
-    for d in range(3):
-        value = value + gcx[d, :, 0:HB].astype(F32)
-    gcs[6, :, 0:HB] = value.astype(BF16)
-    gc_z = push(gcs.at[6], gcz, (near_row, c))
-
-    wait_all(q_z)
+            at = v // 2, 2 * (v % 2) + u
+            value = small_term(v, u, core) + ggot[at].astype(F32)
+            gown[at] = value
+            ghalf[at] = value.astype(BF16)
+
+    def small_y(i):
+        off, size = CW[i]
+        return [
+            push(ghalf.at[:, (y + d) % 4, off:off + size, :], gry.at[d - 1, :, off:off + size, :], y_peer(d))
+            for d in (1, 2, 3)
+        ]
+
+    g_y = [small_y(0), small_y(1)]
+
+    for copies in q_z:
+        wait_all(copies)
     value = qyf[:, lanes(256 * zhi, 256)]
     for d in range(3):
         value = value + qrz[d].astype(F32)
@@ -389,6 +445,18 @@
     for u in range(2):
         hs[:, 64 * u:64 * u + 64, 0:320] = hfull[:, rows(64 * (2 * u + far), 64), 0:320].astype(BF16)
     h_core = push(hs, hc, core_peer)
+    cols_near.relay()
+    h_core.wait_recv()
+    for v in range(8):
+        for u in range(2):
+            value = hfull[v, rows(64 * (2 * u + core), 64), 0:320] + hc[v, 64 * u:64 * u + 64, 0:320].astype(F32)
+            hyf[v, u, :, 0:320] = value
+            hh[v, u, :, 0:320] = value.astype(BF16)
+    h_r = [push(hh.at[(r + d) % 8], hr.at[d - 1], row_peer(d)) for d in range(1, 8)]
+
+    cols_own.start()
+    gcn[...] = cols_term(near_row)
+    gcf[...] = cols_term(r)
 
     def small_z(i):
         off, size = CW[i]
@@ -404,30 +472,23 @@
             for d in (1, 2, 3)
         ]
 
-    h_core.wait_recv()
-    for v in range(8):
-        for u in range(2):
-            at = slice(64 * u, 64 * u + 64)
-            value = hfull[v, rows(64 * (2 * u + core), 64), 0:320] + hc[v, at, 0:320].astype(F32)
-            hfull[v, rows(64 * (2 * u + core), 64), 0:320] = value
-            hh[u, v, :, 0:320] = value.astype(BF16)
-    h_pair = push(hh.at[1 - yl], hy, pair_peer)
-
     g_z = [small_z(0)]
 
-    h_pair.wait_recv()
-    for v in range(8):
-        value = hfull[v, rows(64 * kn, 64), 0:320] + hy[v, :, 0:320].astype(F32)
-        hyf[v, :, 0:320] = value
-        hys[v, :, 0:320] = value.astype(BF16)
-    h_r = [push(hys.at[(r + d) % 8], hr.at[d - 1], row_peer(d)) for d in range(1, 8)]
-
+    gce[:, 0:HB] = cols_near.result(gcn[...]).astype(BF16)
+    gc_z = push(gce, gcz, (near_row, c))
+
+    wait_all(h_r)
+    for u in range(2):
+        value = hyf[r, u, :, 0:320]
+        for d in range(7):
+            value = value + hr[d, u, :, 0:320].astype(F32)
+        hp[u, :, 0:320] = value
+        hq[u, :, 0:320] = value.astype(BF16)
+    h_pair = push(hq.at[1 - yl], hy, pair_peer)
     g_z.append(small_z(1))
-
-    wait_all(gc_x[3:6])
-    value = gcf[...]
-    for d in range(3):
-        value = value + gcx[3 + d, :, 0:HB].astype(F32)
+    cols_own.relay()
+
+    value = cols_own.result(gcf[...])
     gc_z.wait_recv()
     value = (value + gcz[:, 0:HB].astype(F32)).astype(BF16)
     for k in range(4):
@@ -435,11 +496,8 @@
     gc_copy = pltpu.make_async_copy(gc, gc_out, lsem.at[5])
     gc_copy.start()
 
-    wait_all(h_r)
-    value = hyf[r, :, 0:320]
-    for d in range(7):
-        value = value + hr[d, :, 0:320].astype(F32)
-    gr_out[...] = value.astype(BF16)
+    h_pair.wait_recv()
+    gr_out[...] = (hp[yl, :, 0:320] + hy[:, 0:320].astype(F32)).astype(BF16)
 
     for copies in g_z:
         wait_all(copies)
@@ -454,6 +512,12 @@
             copy.wait_send()
         else:
             pl.when(cond)(copy.wait_send)
+
+
+def store(gr, gc, gs, gr_out, gc_out, gs_out):
+    gr_out[...] = gr[...]
+    gc_out[...] = gc[...]
+    gs_out[...] = gs[...]
 
 
 def local(activations, cotangent, small_weight, grow_rows, grow_cols):
@@ -469,19 +533,20 @@
         bf(3, HP, 1024), f32(HP, 1024), bf(HP, 1024), bf(3, HP, 256), bf(256, 128),
         bf(4, 4, HW, 256), bf(4, 4, HW, 256), f32(4, 4, HW, 256), bf(4, 4, HW, 256),
         bf(3, 4, HW, 256), f32(4, HW, 256), bf(4, HW, 256), bf(3, HW, 256),
-        bf(7, FP, LB), bf(6, FP, LB), f32(FP, HB), f32(FP, HB), bf(FP, LB),
-        f32(8, 256, LA), bf(8, 128, LA), bf(8, 128, LA), bf(2, 8, 64, LA), bf(8, 64, LA),
-        f32(8, 64, LA), bf(8, 64, LA), bf(7, 64, LA),
+        bf(2, 3, FP, LB), bf(2, 2, FP, LB), bf(2, 2, 112, LB), bf(FP, LB), f32(FP, HB), f32(FP, HB), bf(FP, LB),
+        f32(8, 256, LA), bf(8, 128, LA), bf(8, 128, LA), bf(8, 2, 64, LA), f32(8, 2, 64, LA),
+        bf(7, 2, 64, LA), f32(2, 64, LA), bf(2, 64, LA), bf(64, LA),
         pltpu.SemaphoreType.DMA((NSEM,)), pltpu.SemaphoreType.DMA((NSEM,)), pltpu.SemaphoreType.DMA((6,)),
     ]
     vmem, hbm = pl.BlockSpec(memory_space=pltpu.VMEM), pl.BlockSpec(memory_space=pl.ANY)
-    gr, gc, gs = pl.pallas_call(
+    out_shape = (
+        jax.ShapeDtypeStruct((64, 320), BF16),
+        jax.ShapeDtypeStruct((216, 688), BF16),
+        jax.ShapeDtypeStruct((172, 256), BF16),
+    )
+    results = pl.pallas_call(
         functools.partial(kernel, scale),
-        out_shape=(
-            jax.ShapeDtypeStruct((64, 320), BF16),
-            jax.ShapeDtypeStruct((216, 688), BF16),
-            jax.ShapeDtypeStruct((172, 256), BF16),
-        ),
+        out_shape=out_shape,
         in_specs=[hbm] * 5,
         out_specs=(vmem, hbm, vmem),
         scratch_shapes=scratch,
@@ -491,6 +556,13 @@
         cost_estimate=pl.CostEstimate(flops=3_700_000_000, bytes_accessed=3_000_000, transcendentals=110_592),
         name="grow",
     )(activations.T, cotangent.T, small_weight.T, grow_rows.T, grow_cols)
+    gr, gc, gs = pl.pallas_call(
+        store,
+        out_shape=out_shape,
+        in_specs=[vmem] * 3,
+        out_specs=(vmem,) * 3,
+        name="store",
+    )(*results)
     return gr.T, gc, gs.T
 
 

time: 145 us -> 138 us (0.952)
  local copies, waits for them, and re-layouts: 3.82 us -> 0 us
  Pallas kernels: 138 us -> 135 us
    unnamed x5 -> x0, local copies, waits for them, and re-layouts: 3.82 us -> none
    pallas_call x1 -> x2, Pallas kernels: 138 us -> 135 us  [the longest x1 133 us: local(): pl.pallas_call(functools.partial(kernel, scale), out_shape=out_shape, in_...]
where the time goes in v4:
time: 138 us; the launch traced here: 136 us
  Pallas kernels  135 us (98%)
    pallas_call x1, Pallas kernels, local(): pl.pallas_call(functools.partial(kernel, scale), out_shape=out_shape, in_...  133 us

profile of v4, /device:TPU:33, one launch (start us, length us, event | category | flops | bytes accessed | tf_op | source)
XLA Modules:
  0.0 135.7 jit_solution(2936836153565541599)
XLA Ops:
  0.6 133.3 %grow.1 = (bf16[64,320]{1,0:T(8,128)(2,1)}, bf16[216,688]{1,0:T(8,128)(2,1)}, bf16[172,256]{1,0:T(8,128)(2,1)}) custom-call(bf16[320,128]{1,0:T(8,128)(2,1)} %bitcast.9, bf16[216,512]{1,0:T(8,128)(2,1)} %bitcast.6, bf16[172,256]{1,0:T(8,128)(2,1)} %bitcast.7, bf16[64,320]{1,0:T(8,128)(2,1)} %bitcast.10, bf16[216,688]{1,0:T(8,128)(2,1)} %b_in.1), custom_call_target="tpu_custom_call" | custom-call | flops 3700000000 | bytes 3000000 | tf_op jit(solution)/shard_map/grow/pallas_call | solution.py:547
  133.9 1.8 %store.1 = (bf16[64,320]{1,0:T(8,128)(2,1)}, bf16[216,688]{1,0:T(8,128)(2,1)}, bf16[172,256]{1,0:T(8,128)(2,1)}) custom-call(bf16[64,320]{1,0:T(8,128)(2,1)} %get-tuple-element.9.gr, bf16[216,688]{1,0:T(8,128)(2,1)} %get-tuple-element.10.gc, bf16[172,256]{1,0:T(8,128)(2,1)} %get-tuple-element.11.gs), custom_call_target="tpu_custom_call" | custom-call | tf_op jit(solution)/shard_map/store/pallas_call | solution.py:559

commit v5 on v4

--- a/solution.py
+++ b/solution.py
@@ -124,7 +124,7 @@
     loads[1].wait()
     wpad[0:172, :] = w[...]
     wpad[172:HW, :] = jnp.zeros((HW - 172, 256), BF16)
-    wbuf[zhi, rows(HW * (2 * y + core), HW), :] = wpad[...]
+    wbuf[0, rows(HW * (2 * y + core), HW), :] = wpad[...]
     loads[2].wait()
     apad[:, 0:320] = a[...]
     apad[:, 320:LA] = jnp.zeros((64, LA - 320), BF16)
@@ -186,24 +186,25 @@
             wait_all(self.rest)
 
     class ColGather:
-        def __init__(self, at, band):
-            self.at, self.band = at, band
+        def __init__(self, at, rest, band):
+            self.at, self.rest, self.band = at, rest, band
             self.y, self.core = [], []
 
         def start(self):
-            block = self.at(zhi)
-            self.z = [push(block, block, z_peer(d)) for d in (1, 2, 3)]
-
-        def along_y(self, e):
-            if e:
-                self.z[e - 1].wait_recv()
-            block = self.at((zhi + 4 - e) % 4)
+            self.z = [push(self.at(0), self.at(4 - d), z_peer(d)) for d in (1, 2, 3)]
+
+        def own_y(self):
+            block = self.at(0)
             self.y.append([push(block, block, y_peer(d)) for d in (1, 2, 3)])
+
+        def rest_y(self):
+            wait_all(self.z)
+            self.y.append([push(self.rest, self.rest, y_peer(d)) for d in (1, 2, 3)])
 
         def to_core(self, d):
             if d:
-                for e in range(4):
-                    self.y[e][d - 1].wait_recv()
+                for copies in self.y:
+                    copies[d - 1].wait_recv()
             block = self.band((y + 4 - d) % 4)
             self.core.append(push(block, block, core_peer))
 
@@ -211,7 +212,8 @@
             wait_all(self.core)
 
     gather_w = ColGather(
-        lambda z: wbuf.at[z, rows(HW * (2 * y + core), HW), :],
+        lambda e: wbuf.at[e, rows(HW * (2 * y + core), HW), :],
+        wbuf.at[1:4, rows(HW * (2 * y + core), HW), :],
         lambda other: wbuf.at[:, rows(HW * (2 * other + core), HW), :])
     gather_a = RowGather(lambda row: abuf.at[acore, lanes(LA * row, LA)])
     b_parts = (lambda row: bbuf.at[row, 0:FP, :]), (lambda row, i: bbuf.at[row, 112 * i:112 * i + 112, :])
@@ -249,8 +251,9 @@
 
     a_block = abuf.at[arow, lanes(LA * r, LA)]
     a_pair = push(a_block, a_block, pair_peer)
-    gather_w.along_y(0)
+    gather_w.own_y()
     gather_b.relay()
+    gather_w.start()
     a_pair.wait_recv()
     gather_a.start_near()
     gather_a.start()
@@ -260,11 +263,9 @@
     bt[...] = jnp.zeros_like(bt)
     act_wait()
     act_y = push(axb.at[yh], axb.at[yh], y_peer(2))
-    gather_w.start()
+    gather_w.rest_y()
     gather_a.forward()
     gather_bn.relay()
-    for e in (1, 2, 3):
-        gather_w.along_y(e)
     gather_a.finish()
     a_core = push(abuf.at[acore, :], abuf.at[acore, :], core_peer)
 
@@ -274,24 +275,24 @@
     for v in range(1, 8):
         total = total + nn(abuf[:, LA * v:LA * v + 320], axb[v % 2, v // 2])
     prow = rows(HP * kt, HP)
-    pbuf[prow, lanes(1024 * yh + 256 * zhi, 256)] = jnp.concatenate(
+    pbuf[prow, lanes(1024 * yh, 256)] = jnp.concatenate(
         [total[0:64], total[128:192], total[64:128], total[192:256]], axis=0).T.astype(BF16)
     gather_p = ColGather(
-        lambda z: pbuf.at[prow, lanes(1024 * yh + 256 * z, 256)],
+        lambda e: pbuf.at[prow, lanes(1024 * yh + 256 * e, 256)],
+        pbuf.at[prow, lanes(1024 * yh + 256, 768)],
         lambda other: pbuf.at[rows(HP * (2 * core + other % 2), HP), lanes(1024 * (other // 2), 1024)])
     gather_p.start()
-    gather_p.along_y(0)
+    gather_p.own_y()
     for d in range(4):
         gather_w.to_core(d)
-    for e in (1, 2, 3):
-        gather_p.along_y(e)
+    gather_p.rest_y()
     gather_p.to_core(0)
 
     def chain_term(row):
-        return nn(bbuf[row, 0:FP, 0:HB], wbuf[row // 2, rows(HB * (row % 2), HB), :])
+        return nn(bbuf[row, 0:FP, 0:HB], wbuf[(row // 2 + 4 - zhi) % 4, rows(HB * (row % 2), HB), :])
 
     def panel(row):
-        return lanes(1024 * (row % 2) + 256 * (row // 2), 256)
+        return lanes(1024 * (row % 2) + 256 * ((row // 2 + 4 - zhi) % 4), 256)
 
     own = panel(r)
     gather_w.finish()
@@ -302,17 +303,15 @@
         total = total + chain_term((r + 2 * d) % 8) + chain_term((near_row + 2 * d) % 8)
     ct[:, own] = total.astype(BF16)
     gather_c = RowGather(lambda row: ct.at[:, panel(row)])
-    gather_c.start_near()
-    gather_c.start()
-
-    gather_c.forward()
+    c_ag = [push(ct.at[:, own], ct.at[:, own], row_peer(d)) for d in range(1, 8)]
+
     for v in range(8):
         bbuft[v] = bbuf[v].T
     for d in (1, 2, 3):
         gather_p.to_core(d)
     gather_p.finish()
     loads[4].wait()
-    gather_c.finish()
+    wait_all(c_ag)
 
     for k in range(4):
         t = KT[k]
@@ -357,7 +356,7 @@
     bt[0:FP, :] = (back * scale).astype(BF16)
 
     def cols_term(row):
-        return nt(bt[0:FP, :], wbuf[row // 2, rows(HB * (row % 2), HB), :])
+        return nt(bt[0:FP, :], wbuf[(row // 2 + 4 - zhi) % 4, rows(HB * (row % 2), HB), :])
 
     class RingSum:
         def __init__(self, i, row):
@@ -391,6 +390,7 @@
             return value + gcx[self.i, 0, :, 0:HB].astype(F32) + gcx[self.i, 1, :, 0:HB].astype(F32)
 
     cols_near, cols_own = RingSum(0, near_row), RingSum(1, r)
+    cols_near.start()
 
     def small_term(v, u, which):
         return nn(bbuft[v, rows(HW * (2 * u + which), HW), :], bt[...])
@@ -412,11 +412,11 @@
             qyf[part, at] = value
             qys[part, at] = value.astype(BF16)
         q_z.append([
-            push(qys.at[part, lanes(256 * ((zhi + d) % 4), 256)], qrz.at[d - 1, part, :], z_peer(d))
+            push(qys.at[part, 256 * d:256 * d + 256], qrz.at[d - 1, part, :], z_peer(d))
             for d in (1, 2, 3)
         ])
 
-    cols_near.start()
+    cols_own.start()
     g_core.wait_recv()
     for v in range(8):
         for u in range(2):
@@ -433,10 +433,11 @@
         ]
 
     g_y = [small_y(0), small_y(1)]
+    cols_near.relay()
 
     for copies in q_z:
         wait_all(copies)
-    value = qyf[:, lanes(256 * zhi, 256)]
+    value = qyf[:, 0:256]
     for d in range(3):
         value = value + qrz[d].astype(F32)
     qt[...] = (value * scale).T.astype(BF16)
@@ -445,7 +446,6 @@
     for u in range(2):
         hs[:, 64 * u:64 * u + 64, 0:320] = hfull[:, rows(64 * (2 * u + far), 64), 0:320].astype(BF16)
     h_core = push(hs, hc, core_peer)
-    cols_near.relay()
     h_core.wait_recv()
     for v in range(8):
         for u in range(2):
@@ -454,7 +454,7 @@
             hh[v, u, :, 0:320] = value.astype(BF16)
     h_r = [push(hh.at[(r + d) % 8], hr.at[d - 1], row_peer(d)) for d in range(1, 8)]
 
-    cols_own.start()
+    cols_own.relay()
     gcn[...] = cols_term(near_row)
     gcf[...] = cols_term(r)
 
@@ -486,7 +486,6 @@
         hq[u, :, 0:320] = value.astype(BF16)
     h_pair = push(hq.at[1 - yl], hy, pair_peer)
     g_z.append(small_z(1))
-    cols_own.relay()
 
     value = cols_own.result(gcf[...])
     gc_z.wait_recv()

time: 138 us -> 135 us (0.978)
  Pallas kernels: 135 us -> 132 us
    pallas_call x1, Pallas kernels: 133 us -> 131 us  [local(): pl.pallas_call(functools.partial(kernel, scale), out_shape=out_shape, in_...]
where the time goes in v5:
time: 135 us; the launch traced here: 133 us
  Pallas kernels  132 us (98%)
    pallas_call x1, Pallas kernels, local(): pl.pallas_call(functools.partial(kernel, scale), out_shape=out_shape, in_...  131 us

profile of v5, /device:TPU:33, one launch (start us, length us, event | category | flops | bytes accessed | tf_op | source)
XLA Modules:
  0.0 133.0 jit_solution(6550373068703128764)
XLA Ops:
  0.6 130.6 %grow.1 = (bf16[64,320]{1,0:T(8,128)(2,1)}, bf16[216,688]{1,0:T(8,128)(2,1)}, bf16[172,256]{1,0:T(8,128)(2,1)}) custom-call(bf16[320,128]{1,0:T(8,128)(2,1)} %bitcast.9, bf16[216,512]{1,0:T(8,128)(2,1)} %bitcast.6, bf16[172,256]{1,0:T(8,128)(2,1)} %bitcast.7, bf16[64,320]{1,0:T(8,128)(2,1)} %bitcast.10, bf16[216,688]{1,0:T(8,128)(2,1)} %b_in.1), custom_call_target="tpu_custom_call" | custom-call | flops 3700000000 | bytes 3000000 | tf_op jit(solution)/shard_map/grow/pallas_call | solution.py:546
  131.2 1.8 %store.1 = (bf16[64,320]{1,0:T(8,128)(2,1)}, bf16[216,688]{1,0:T(8,128)(2,1)}, bf16[172,256]{1,0:T(8,128)(2,1)}) custom-call(bf16[64,320]{1,0:T(8,128)(2,1)} %get-tuple-element.9.gr, bf16[216,688]{1,0:T(8,128)(2,1)} %get-tuple-element.10.gc, bf16[172,256]{1,0:T(8,128)(2,1)} %get-tuple-element.11.gs), custom_call_target="tpu_custom_call" | custom-call | tf_op jit(solution)/shard_map/store/pallas_call | solution.py:558

commit v6 on v5

--- a/solution.py
+++ b/solution.py
@@ -19,7 +19,7 @@
 NSEM = 256
 KT = (0, 2, 1, 3)
 CW = ((0, 96), (96, 80))
-CQ = ((0, 64), (64, 64))
+CQ = ((0, 32), (32, 32), (64, 32), (96, 32))
 
 
 def nn(a, b):

time: 135 us -> 134 us (level)
  no operation moved by 1% of the time
where the time goes in v6:
time: 134 us; the launch traced here: 132 us
  Pallas kernels  131 us (98%)
    pallas_call x1, Pallas kernels, local(): pl.pallas_call(functools.partial(kernel, scale), out_shape=out_shape, in_...  130 us

profile of v6, /device:TPU:33, one launch (start us, length us, event | category | flops | bytes accessed | tf_op | source)
XLA Modules:
  0.0 132.0 jit_solution(8618340875044646018)
XLA Ops:
  0.6 129.6 %grow.1 = (bf16[64,320]{1,0:T(8,128)(2,1)}, bf16[216,688]{1,0:T(8,128)(2,1)}, bf16[172,256]{1,0:T(8,128)(2,1)}) custom-call(bf16[320,128]{1,0:T(8,128)(2,1)} %bitcast.9, bf16[216,512]{1,0:T(8,128)(2,1)} %bitcast.6, bf16[172,256]{1,0:T(8,128)(2,1)} %bitcast.7, bf16[64,320]{1,0:T(8,128)(2,1)} %bitcast.10, bf16[216,688]{1,0:T(8,128)(2,1)} %b_in.1), custom_call_target="tpu_custom_call" | custom-call | flops 3700000000 | bytes 3000000 | tf_op jit(solution)/shard_map/grow/pallas_call | solution.py:546
  130.2 1.8 %store.1 = (bf16[64,320]{1,0:T(8,128)(2,1)}, bf16[216,688]{1,0:T(8,128)(2,1)}, bf16[172,256]{1,0:T(8,128)(2,1)}) custom-call(bf16[64,320]{1,0:T(8,128)(2,1)} %get-tuple-element.9.gr, bf16[216,688]{1,0:T(8,128)(2,1)} %get-tuple-element.10.gc, bf16[172,256]{1,0:T(8,128)(2,1)} %get-tuple-element.11.gs), custom_call_target="tpu_custom_call" | custom-call | tf_op jit(solution)/shard_map/store/pallas_call | solution.py:558
